TPU v7x, 128 devices: a whole 4x4x4 slice. The times are simulated.
128 devices in a mesh: grp: 8 (over y, core), tp: 16 (over z, x).
Axes of the slice: x: 4, y: 4, z: 4, core: 2. Of those that a mesh axis runs over, the one named last changes fastest.
Arguments:
- prefill_x: bfloat16 [2048, 8192], P('grp', 'tp'), may hold values from -6 to 6
- span_index: int32 [8], replicated, may hold values from 0 to 7, as said below
- prefix_pages: int32 [8, 112], P('grp'), may hold values from 0 to 111, each once within a row
- prefix_cache: bfloat16 [8, 16, 1792, 256], P('grp', 'tp'), may hold values from -300 to 300, as said below
- decode_x: bfloat16 [2, 512, 8192], P(None, 'grp', 'tp'), may hold values from -6 to 6
- decode_len: int32 [8, 2, 32], P('grp'), may hold values from 1 to 512, 8192 in all within a row
- page_order: int32 [8, 2, 544], P('grp'), may hold values from 0 to 543, each once within a row
- assignment: int32 [8], replicated, may hold values from 0 to 7
- kv_cache: bfloat16 [8, 16, 8704, 256], P('grp', 'tp'), may hold values from -300 to 300
- w_query: bfloat16 [8192, 8192], P(None, 'tp'), may hold values from -0.0625 to 0.0625
- w_keyval: bfloat16 [8192, 2048], P(None, 'tp'), may hold values from -0.0625 to 0.0625
- w_out: bfloat16 [8192, 8192], P('tp'), may hold values from -0.0625 to 0.0625
Outputs:
- prefill_out: bfloat16 [2048, 8192], P('grp', 'tp')
- decode_out: bfloat16 [2, 512, 8192], P(None, 'grp', 'tp')
Inputs may be any that keep to these rules, and one draw needn't show every extreme that they name: `span_index`: exactly 4 prompts are at span 8 - 1, and one prompt is at span 0. `prefix_pages`: each row holds every page number of its prefix pool once. `prefix_cache`: the pools h * 2 + m of one group are equal for every m < 2. `decode_len`: each row of 32 lengths sums to 8192, and its largest is 512. `page_order`: each row holds every page number of its pool once.
All inputs are finite; a program needn't handle non-finite values.
Results may differ from a plain program's by a relative error of at most 0.019.
Values may be sent and summed in bfloat16 or wider, within the bound.
A program may use at most 128 MiB of HBM per device.

v0:
```python
import jax
import jax.numpy as jnp
from jax import lax
from jax.sharding import PartitionSpec as P

KV_HEADS = 8
HEAD_DIM = 128
SPANS = 8
PAGE = 16
MAX_PAGES = 32


rope_base = 500000.0
masked_score = -1e30


def from_partner(value, axis, distance):
    mask = 2**distance
    pairs = [(source, source ^ mask) for source in range(lax.axis_size(axis))]
    return lax.ppermute(value, axis, pairs)


def rotary(values, positions):
    half = values.shape[-1] // 2
    exponent = jnp.arange(half, dtype=jnp.float32) * (2.0 / values.shape[-1])
    angles = positions.astype(jnp.float32)[..., None] * rope_base ** (-exponent)
    cosine = jnp.cos(angles)
    sine = jnp.sin(angles)
    first = values[..., :half]
    second = values[..., half:]
    return jnp.concatenate([first * cosine - second * sine, second * cosine + first * sine], -1)


def ordered(mine, theirs, member, axis):
    return jnp.where(
        member == 0, jnp.concatenate([mine, theirs], axis), jnp.concatenate([theirs, mine], axis)
    )


def body(
    prefill_x,
    span_index,
    prefix_pages,
    prefix_cache,
    decode_x,
    decode_len,
    page_order,
    assignment,
    kv_cache,
    w_query,
    w_keyval,
    w_out,
):
    split = lax.axis_size("tp") // KV_HEADS
    member = lax.axis_index("tp") % split
    group = lax.axis_index("grp")
    prompts = lax.axis_size("grp")
    span = prefill_x.shape[0]
    decode = decode_x.shape[1]
    dec_dev = decode // split
    heads_dev = w_query.shape[1] // HEAD_DIM
    pre_rows = prefix_cache.shape[2]
    context_rows = pre_rows + span
    scale = HEAD_DIM ** (-0.5)

    def accumulate(piece):
        return (
            jnp.dot(piece, w_query, preferred_element_type=jnp.float32),
            jnp.dot(piece, w_keyval, preferred_element_type=jnp.float32),
        )

    pre_query, pre_pair = accumulate(lax.all_gather(prefill_x, "tp", axis=1, tiled=True))
    pre_half = pre_pair.astype(jnp.bfloat16)
    pre_whole = ordered(pre_half, from_partner(pre_half, "tp", 0), member, 1)
    start_row = span_index[group] * span
    pre_spots = start_row + jnp.arange(span, dtype=jnp.int32)
    queries = rotary(pre_query.reshape(span, heads_dev, HEAD_DIM), pre_spots[:, None]).astype(
        jnp.bfloat16
    )
    pre_keys = rotary(pre_whole[:, :HEAD_DIM].astype(jnp.float32), pre_spots).astype(jnp.bfloat16)
    pre_values = pre_whole[:, HEAD_DIM:]
    prior_pool = prefix_cache.reshape(-1, PAGE, 2 * HEAD_DIM)
    prior = prior_pool[prefix_pages[0]].reshape(pre_rows, 2 * HEAD_DIM)
    prior_scores = (
        jnp.einsum("qhd,kd->hqk", queries, prior[:, :HEAD_DIM], preferred_element_type=jnp.float32)
        * scale
    )
    prior_live = jnp.arange(pre_rows, dtype=jnp.int32) < start_row
    prior_scores = jnp.where(prior_live[None, None, :], prior_scores, masked_score)
    own_scores = (
        jnp.einsum("qhd,kd->hqk", queries, pre_keys, preferred_element_type=jnp.float32) * scale
    )
    causal = jnp.arange(span)[:, None] >= jnp.arange(span)[None, :]
    own_scores = jnp.where(causal[None], own_scores, masked_score)
    highest = jnp.maximum(jnp.max(prior_scores, -1), jnp.max(own_scores, -1))[..., None]
    prior_raised = jnp.exp(prior_scores - highest)
    own_raised = jnp.exp(own_scores - highest)
    totals = (jnp.sum(prior_raised, -1) + jnp.sum(own_raised, -1))[..., None]
    prior_weights = (prior_raised / totals).astype(jnp.bfloat16)
    own_weights = (own_raised / totals).astype(jnp.bfloat16)
    pre_heads = jnp.einsum(
        "hqk,kd->qhd", prior_weights, prior[:, HEAD_DIM:], preferred_element_type=jnp.float32
    )
    pre_heads = pre_heads + jnp.einsum(
        "hqk,kd->qhd", own_weights, pre_values, preferred_element_type=jnp.float32
    )
    pre_heads = pre_heads.astype(jnp.bfloat16).reshape(span, heads_dev * HEAD_DIM)
    pre_terms = jnp.dot(pre_heads, w_out, preferred_element_type=jnp.float32)
    finished = span_index == SPANS - 1
    sources = jnp.arange(prompts, dtype=jnp.int32)
    target = assignment[group]
    sent_there = (assignment == target) & finished
    target_rank = jnp.sum(sent_there & (sources < group))
    outgoing_rows = jnp.concatenate([prior, jnp.concatenate([pre_keys, pre_values], 1)], 0)
    to_here = (assignment == group) & finished
    ranks = jnp.sum(to_here[None, :] & (sources[None, :] < sources[:, None]), 1)
    owner = ranks % split * dec_dev + ranks // split
    wanted = to_here & (ranks % split == member)
    chosen = (sources == target) & finished[group] & (target_rank % split == member)
    outgoing = jnp.where(
        chosen[:, None, None], outgoing_rows[None], jnp.zeros_like(outgoing_rows)[None]
    )
    arrived = lax.all_to_all(outgoing, "grp", split_axis=0, concat_axis=0, tiled=True)
    rows = 2 * decode
    dec_query, dec_pair = accumulate(
        lax.all_gather(decode_x.reshape(rows, decode_x.shape[2]), "tp", axis=1, tiled=True)
    )
    dec_half = dec_pair.astype(jnp.bfloat16)
    dec_whole = ordered(dec_half, from_partner(dec_half, "tp", 0), member, 1)
    all_lengths = decode_len.reshape(decode)
    sequence_ids = jnp.arange(decode, dtype=jnp.int32)
    owned_all = jnp.any((owner[None, :] == sequence_ids[:, None]) & to_here[None, :], 1)
    base = jnp.where(owned_all, context_rows, all_lengths)
    spots = base[None, :] + jnp.arange(2, dtype=jnp.int32)[:, None]
    dec_queries = rotary(
        dec_query.reshape(2, decode, heads_dev, HEAD_DIM), spots[:, :, None]
    ).astype(jnp.bfloat16)
    new_keys = rotary(
        dec_whole[:, :HEAD_DIM].astype(jnp.float32).reshape(2, decode, HEAD_DIM), spots
    ).astype(jnp.bfloat16)
    new_values = dec_whole[:, HEAD_DIM:].reshape(2, decode, HEAD_DIM)
    block_queries = dec_queries.reshape(2, split, dec_dev, heads_dev, HEAD_DIM)
    mine = lax.dynamic_index_in_dim(block_queries, member, 1, keepdims=False)
    others = lax.dynamic_index_in_dim(block_queries, 1 - member, 1, keepdims=False)
    group_queries = ordered(mine, from_partner(others, "tp", 0), member, 2)
    my_keys = lax.dynamic_index_in_dim(
        new_keys.reshape(2, split, dec_dev, HEAD_DIM), member, 1, keepdims=False
    )
    my_values = lax.dynamic_index_in_dim(
        new_values.reshape(2, split, dec_dev, HEAD_DIM), member, 1, keepdims=False
    )
    my_lengths = lax.dynamic_index_in_dim(decode_len[0], member, 0, keepdims=False)
    my_order = lax.dynamic_index_in_dim(page_order[0], member, 0, keepdims=False)
    pool_dev = my_order.shape[0]
    counts = (my_lengths + PAGE - 1) // PAGE
    firsts = jnp.cumsum(counts) - counts
    slots = jnp.clip(
        firsts[:, None] + jnp.arange(MAX_PAGES, dtype=jnp.int32)[None, :], 0, pool_dev - 1
    )
    page_ids = my_order[slots]
    pool = kv_cache.reshape(pool_dev, PAGE, 2 * HEAD_DIM)
    cached = pool[page_ids].reshape(dec_dev, MAX_PAGES * PAGE, 2 * HEAD_DIM)
    live = jnp.arange(MAX_PAGES * PAGE)[None, :] < my_lengths[:, None]
    step_order = jnp.arange(2)[:, None] >= jnp.arange(2)[None, :]
    pool_scores = (
        jnp.einsum(
            "tjgd,jcd->jtgc",
            group_queries,
            cached[..., :HEAD_DIM],
            preferred_element_type=jnp.float32,
        )
        * scale
    )
    pool_scores = jnp.where(live[:, None, None, :], pool_scores, masked_score)
    fresh_scores = (
        jnp.einsum("tjgd,ujd->jtgu", group_queries, my_keys, preferred_element_type=jnp.float32)
        * scale
    )
    fresh_scores = jnp.where(step_order[None, :, None, :], fresh_scores, masked_score)
    highest = jnp.maximum(jnp.max(pool_scores, -1), jnp.max(fresh_scores, -1))[..., None]
    pool_raised = jnp.exp(pool_scores - highest)
    fresh_raised = jnp.exp(fresh_scores - highest)
    totals = (jnp.sum(pool_raised, -1) + jnp.sum(fresh_raised, -1))[..., None]
    pool_weights = (pool_raised / totals).astype(jnp.bfloat16)
    fresh_weights = (fresh_raised / totals).astype(jnp.bfloat16)
    attended = jnp.einsum(
        "jtgc,jcd->tjgd", pool_weights, cached[..., HEAD_DIM:], preferred_element_type=jnp.float32
    )
    attended = attended + jnp.einsum(
        "jtgu,ujd->tjgd", fresh_weights, my_values, preferred_element_type=jnp.float32
    )
    attended = attended.astype(jnp.bfloat16)
    local_slots = jnp.arange(dec_dev, dtype=jnp.int32)
    picks = (wanted[:, None] & ((ranks // split)[:, None] == local_slots[None, :])).astype(
        jnp.bfloat16
    )
    source_queries = jnp.einsum(
        "sj,tjgd->tsgd", picks, group_queries, preferred_element_type=jnp.float32
    ).astype(jnp.bfloat16)
    source_keys = jnp.einsum(
        "sj,ujd->usd", picks, my_keys, preferred_element_type=jnp.float32
    ).astype(jnp.bfloat16)
    source_values = jnp.einsum(
        "sj,ujd->usd", picks, my_values, preferred_element_type=jnp.float32
    ).astype(jnp.bfloat16)
    context_scores = (
        jnp.einsum(
            "tsgd,scd->stgc",
            source_queries,
            arrived[..., :HEAD_DIM],
            preferred_element_type=jnp.float32,
        )
        * scale
    )
    step_scores = (
        jnp.einsum(
            "tsgd,usd->stgu", source_queries, source_keys, preferred_element_type=jnp.float32
        )
        * scale
    )
    step_scores = jnp.where(step_order[None, :, None, :], step_scores, masked_score)
    peak = jnp.maximum(jnp.max(context_scores, -1), jnp.max(step_scores, -1))[..., None]
    context_raised = jnp.exp(context_scores - peak)
    step_raised = jnp.exp(step_scores - peak)
    sums = (jnp.sum(context_raised, -1) + jnp.sum(step_raised, -1))[..., None]
    context_weights = (context_raised / sums).astype(jnp.bfloat16)
    step_weights = (step_raised / sums).astype(jnp.bfloat16)
    taken = jnp.einsum(
        "stgc,scd->tsgd",
        context_weights,
        arrived[..., HEAD_DIM:],
        preferred_element_type=jnp.float32,
    )
    taken = taken + jnp.einsum(
        "stgu,usd->tsgd", step_weights, source_values, preferred_element_type=jnp.float32
    )
    taken = taken.astype(jnp.bfloat16)
    placed = jnp.einsum("sj,tsgd->tjgd", picks, taken, preferred_element_type=jnp.float32).astype(
        jnp.bfloat16
    )
    has_context = jnp.sum(picks.astype(jnp.float32), 0) > 0.5
    attended = jnp.where(has_context[None, :, None, None], placed, attended)
    keep_heads = lax.dynamic_slice_in_dim(attended, member * heads_dev, heads_dev, 2)
    away_heads = lax.dynamic_slice_in_dim(attended, (1 - member) * heads_dev, heads_dev, 2)
    own_heads = ordered(keep_heads, from_partner(away_heads, "tp", 0), member, 1)
    dec_terms = jnp.dot(
        own_heads.reshape(rows, heads_dev * HEAD_DIM), w_out, preferred_element_type=jnp.float32
    )
    prefill_out = lax.psum_scatter(
        pre_terms.astype(jnp.bfloat16), "tp", scatter_dimension=1, tiled=True
    )
    decode_out = lax.psum_scatter(
        dec_terms.astype(jnp.bfloat16), "tp", scatter_dimension=1, tiled=True
    )
    return (prefill_out, decode_out.reshape(2, decode, -1))


def solution(mesh):
    placed = (
        P("grp", "tp"),
        P(),
        P("grp", None),
        P("grp", "tp", None, None),
        P(None, "grp", "tp"),
        P("grp", None, None),
        P("grp", None, None),
        P(),
        P("grp", "tp", None, None),
        P(None, "tp"),
        P(None, "tp"),
        P("tp", None),
    )
    return jax.shard_map(
        body,
        mesh=mesh,
        in_specs=placed,
        out_specs=(P("grp", "tp"), P(None, "grp", "tp")),
        check_vma=False,
    )
```

profile of v0, /device:TPU:0, one launch (start us, length us, event | category | flops | bytes accessed | tf_op | source)
XLA Modules:
  0.0 286.6 jit_solution(17995289460525957453)
XLA Ops:
  10.0 2.0 fusion.81
  23.3 4.5 %gather_fusion.1 = s32[1024]{0:T(1024)S(1)} fusion(s32[544]{0:T(1024)S(1)} %fusion.70, s32[1024]{0:T(1024)S(1)} %broadcast_clamp_fusion.1), kind=kCustom, calls=%fused_computation.1 | custom fusion | bytes 12288 | tf_op jit(solution)/shard_map/gather | solution.py:160
  29.4 1.9 gather_fusion
  31.3 39.1 %all-gather.3.cloned.1.call-done = bf16[256,8192]{1,0:T(8,128)(2,1)} async-done(((bf16[256,512]{1,0:T(8,128)(2,1)}), bf16[256,8192]{1,0:T(8,128)(2,1)}) %all-gather.3.cloned.1.call-update) | async-done | bytes 4194320 | tf_op jit(solution)/shard_map/all_gather | solution.py:72
  70.4 7.8 %fusion.99 = f32[256,512]{1,0:T(8,128)} fusion(bf16[256,8192]{1,0:T(8,128)(2,1)} %all-gather.3.cloned.1.call-done, bf16[8192,512]{1,0:T(8,128)(2,1)} %param.21), kind=kOutput, calls=%fused_computation.205 | convolution fusion | flops 2147483648 | bytes 13107200 | tf_op jit(solution)/shard_map/dot_general | solution.py:68
  79.4 3.5 %convolution_convert_fusion.3 = bf16[256,128]{1,0:T(8,128)(2,1)S(1)} fusion(bf16[256,8192]{1,0:T(8,128)(2,1)} %all-gather.3.cloned.1.call-done, bf16[8192,128]{1,0:T(8,128)(2,1)S(1)} %copy-done), kind=kOutput, calls=%fused_computation.32 | convolution fusion | flops 536903680 | bytes 6356992 | tf_op jit(solution)/shard_map/dot_general | solution.py:69
  85.4 1.9 collective-permute-done
  89.3 3.8 %broadcast_select_fusion = bf16[8,2048,256]{2,1,0:T(8,128)(2,1)} fusion(pred[8]{0:T(512)(128)(4,1)S(1)} %and_and_fusion, bf16[2048,256]{1,0:T(8,128)(2,1)S(1)} %maximum_maximum_fusion), kind=kLoop, calls=%fused_computation.5 | loop fusion | flops 4194304 | bytes 9437192 | tf_op jit(solution)/shard_map/jit(_where)/select_n | solution.py:120
  93.1 5.1 %all-to-all-start = ((bf16[8,2048,256]{2,1,0:T(8,128)(2,1)}), bf16[8,2048,256]{2,1,0:T(8,128)(2,1)}, u32[]{:S(2)}, u32[]{:S(2)}) async-start(bf16[8,2048,256]{2,1,0:T(8,128)(2,1)} %broadcast_select_fusion), calls=%async_computation.1 | async-start | bytes 16777216 | tf_op jit(solution)/shard_map/all_to_all | solution.py:123
  102.6 2.0 fusion.1
  104.6 2.3 fusion.6
  107.3 4.5 %convolution_convert_fusion = bf16[256,8192]{1,0:T(8,128)(2,1)} fusion(bf16[256,512]{0,1:T(8,128)(2,1)S(1)} %bitcast.178, bf16[512,8192]{1,0:T(8,128)(2,1)S(1)} %bitcast.164), kind=kOutput, calls=%fused_computation.3 | convolution fusion | flops 2149580800 | bytes 12845056 | tf_op jit(solution)/shard_map/dot_general | solution.py:108
  112.0 12.0 %gather_fusion.2 = bf16[1024,16,256]{2,1,0:T(8,128)(2,1)} fusion(bf16[544,16,256]{2,1,0:T(8,128)(2,1)} %bitcast.169, s32[1024]{0:T(1024)S(1)} %broadcast_clamp_fusion), kind=kCustom, calls=%fused_computation.2 | custom fusion | bytes 16781312 | tf_op jit(solution)/shard_map/gather | solution.py:162
  124.3 2.5 convolution_convert_fusion.4
  128.0 5.3 %fusion.100 = f32[128,512]{1,0:T(8,128)S(1)} fusion(bf16[128,8192]{1,0:T(8,128)(2,1)} %all-gather.5.cloned.1.call-done, bf16[8192,512]{1,0:T(8,128)(2,1)} %param.21), kind=kOutput, calls=%fused_computation.206 | convolution fusion | flops 1073741824 | bytes 10747904 | tf_op jit(solution)/shard_map/dot_general | solution.py:68
  136.3 3.6 %collective-permute-done.1 = bf16[2,32,4,128]{3,2,0,1:T(4,128)(2,1)S(1)} collective-permute-done((bf16[2,32,4,128]{3,2,0,1:T(4,128)(2,1)S(1)}, bf16[2,32,4,128]{3,2,0,1:T(4,128)(2,1)S(1)}, u32[]{:S(2)}, u32[]{:S(2)}) %collective-permute-start.1) | collective-permute-done | bytes 65568 | tf_op jit(solution)/shard_map/ppermute | solution.py:20
  140.7 3.5 %fusion.95 = (f32[32,2,8]{2,1,0:T(2,128)S(1)}, f32[32,2,8,512]{3,2,1,0:T(8,128)S(1)}) fusion(bf16[2,32,8,128]{3,2,0,1:T(8,128)(2,1)S(1)} %maximum_select_fusion.1, bf16[32,512,256]{2,1,0:T(8,128)(2,1)} %bitcast.167, pred[32,512]{1,0:T(8,128)(4,1)S(1)} %iota_compare_fusion.1), kind=kOutput, calls=%fused_computation.201 | convolution fusion | flops 67894784 | bytes 5392384 | tf_op jit(solution)/shard_map/tjgd,jcd->jtgc/dot_general | solution.py:166
  145.6 3.0 %fusion.3 = f32[32,128,2,8]{1,3,2,0:T(8,128)S(1)} fusion(bf16[32,512,256]{2,1,0:T(8,128)(2,1)} %bitcast.168, f32[32,2,8,512]{3,2,1,0:T(8,128)S(1)} %get-tuple-element.37, f32[32,2,8]{2,1,0:T(2,128)S(1)} %add.256, f32[32,2,8]{2,1,0:T(2,128)S(1)} %max.30), kind=kOutput, calls=%fused_computation.15 | convolution fusion | flops 67895296 | bytes 5509120 | tf_op jit(solution)/shard_map/jtgc,jcd->tjgd/dot_general | solution.py:186
  148.6 44.3 %all-to-all-done = bf16[8,2048,256]{2,1,0:T(8,128)(2,1)} async-done(((bf16[8,2048,256]{2,1,0:T(8,128)(2,1)}), bf16[8,2048,256]{2,1,0:T(8,128)(2,1)}, u32[]{:S(2)}, u32[]{:S(2)}) %all-to-all-start) | async-done | bytes 8388640 | tf_op jit(solution)/shard_map/all_to_all | solution.py:123
  192.8 3.6 %fusion.97 = (f32[8,2,8]{2,1,0:T(2,128)S(1)}, f32[8,2,8,2048]{3,2,1,0:T(8,128)S(1)}) fusion(bf16[8,2048,256]{2,1,0:T(8,128)(2,1)} %all-to-all-done, bf16[2,8,8,128]{3,1,2,0:T(8,128)(2,1)S(1)} %fusion.17), kind=kOutput, calls=%fused_computation.203 | convolution fusion | flops 67633024 | bytes 5276160 | tf_op jit(solution)/shard_map/tsgd,scd->stgc/dot_general | solution.py:207
  196.9 3.1 %fusion.5 = f32[8,128,2,8]{1,3,2,0:T(8,128)S(1)} fusion(bf16[8,2048,256]{2,1,0:T(8,128)(2,1)} %all-to-all-done, f32[8,2,8,2048]{3,2,1,0:T(8,128)S(1)} %get-tuple-element.41, f32[8,2,8]{2,1,0:T(2,128)S(1)} %add.249, f32[8,2,8]{2,1,0:T(2,128)S(1)} %max.28), kind=kOutput, calls=%fused_computation.19 | convolution fusion | flops 67895296 | bytes 5309440 | tf_op jit(solution)/shard_map/stgc,scd->tsgd/dot_general | solution.py:228
  201.7 3.2 %collective-permute-done.3 = bf16[2,32,4,128]{3,1,2,0:T(8,128)(2,1)S(1)} collective-permute-done((bf16[2,32,4,128]{3,1,2,0:T(8,128)(2,1)S(1)}, bf16[2,32,4,128]{3,1,2,0:T(8,128)(2,1)S(1)}, u32[]{:S(2)}, u32[]{:S(2)}) %collective-permute-start.3) | collective-permute-done | bytes 65568 | tf_op jit(solution)/shard_map/ppermute | solution.py:20
  205.1 2.6 convolution_convert_fusion.1
  207.8 72.3 %reduce-scatter.5.cloned.1.call-done = bf16[128,512]{1,0:T(8,128)(2,1)} async-done(((bf16[128,8192]{1,0:T(8,128)(2,1)}), bf16[128,512]{1,0:T(8,128)(2,1)}) %reduce-scatter.5.cloned.1.call-update) | async-done | bytes 131088 | tf_op jit(solution)/shard_map/reduce_scatter | solution.py:252
  (137 shorter events, 32.3 us)
Async XLA Ops:
  7.2 72.2 %copy-start = (bf16[8192,128]{1,0:T(8,128)(2,1)S(1)}, bf16[8192,128]{1,0:T(8,128)(2,1)}, u32[]{:S(2)}) copy-start(bf16[8192,128]{1,0:T(8,128)(2,1)} %param.22) | copy-start | bytes 6291460
  7.2 63.2 %all-gather.3.cloned.1.call-start = ((), (), s32[]{:S(2)}) async-start(), calls=%async_computation.3 | async-start | bytes 4456448 | tf_op jit(solution)/shard_map/all_gather | solution.py:72
  7.9 116.4 %all-gather.5.cloned.1.call-start = ((), (), s32[]{:S(2)}) async-start(), calls=%async_computation.5 | async-start | bytes 2228224 | tf_op jit(solution)/shard_map/all_gather | solution.py:126
  16.5 3.8 %copy-start.6 = (pred[8]{0:T(512)(128)(4,1)}, pred[8]{0:T(512)(128)(4,1)S(1)}, u32[]{:S(2)}) copy-start(pred[8]{0:T(512)(128)(4,1)S(1)} %get-tuple-element.31) | copy-start | bytes 28
  79.4 8.0 %copy-start.12 = (f32[64]{0:T(128)S(1)}, f32[64]{0:T(128)}, u32[]{:S(2)}) copy-start(f32[64]{0:T(128)} %negate_power_fusion) | copy-start | bytes 772
  79.4 8.0 %copy-start.14 = (f32[256]{0:T(256)S(1)}, f32[256]{0:T(256)}, u32[]{:S(2)}) copy-start(f32[256]{0:T(256)} %add_convert_fusion.5) | copy-start | bytes 3076
  82.9 4.4 %collective-permute-start = (bf16[256,128]{1,0:T(8,128)(2,1)S(1)}, bf16[256,128]{1,0:T(8,128)(2,1)S(1)}, u32[]{:S(2)}, u32[]{:S(2)}) collective-permute-start(bf16[256,128]{1,0:T(8,128)(2,1)S(1)} %convolution_convert_fusion.3), channel_id=1, source_target_pairs={{0,1},{1,0},{2,3},{3,2},{4,5},{5,4},{6,7},{7,6},{8,9},{9,8},{10,11... | collective-permute-start | bytes 196616 | tf_op jit(solution)/shard_map/ppermute | solution.py:20
  93.1 5.3 %copy-start.1 = (f32[256,4,64]{2,1,0:T(4,128)S(1)}, f32[256,4,64]{2,1,0:T(4,128)}, u32[]{:S(2)}) copy-start(f32[256,4,64]{2,1,0:T(4,128)} %get-tuple-element.10) | copy-start | bytes 786436
  93.1 99.7 %all-to-all-start = ((bf16[8,2048,256]{2,1,0:T(8,128)(2,1)}), bf16[8,2048,256]{2,1,0:T(8,128)(2,1)}, u32[]{:S(2)}, u32[]{:S(2)}) async-start(bf16[8,2048,256]{2,1,0:T(8,128)(2,1)} %broadcast_select_fusion), calls=%async_computation.1 | async-start | bytes 16777216 | tf_op jit(solution)/shard_map/all_to_all | solution.py:123
  98.2 109.5 %reduce-scatter.3.cloned.1.call-start = ((), (), s32[]{:S(2)}) async-start(), calls=%async_computation.4 | async-start | bytes 4456448 | tf_op jit(solution)/shard_map/reduce_scatter | solution.py:249
  102.5 4.7 %slice-start = ((s8[8388608]{0:T(1024)(128)(4,1)}), s8[4194304]{0:T(1024)(128)(4,1)S(1)}, s32[]{:S(2)}) async-start(s8[8388608]{0:T(1024)(128)(4,1)} %bitcast.163), calls=%async_computation.7 | async-start | bytes 8388608
  104.6 2.6 slice-start.1
  107.3 4.6 %copy-start.15 = (s32[1,2,32]{2,1,0:T(2,128)S(1)}, s32[1,2,32]{2,1,0:T(2,128)}, u32[]{:S(2)}) copy-start(s32[1,2,32]{2,1,0:T(2,128)} %param.17) | copy-start | bytes 772
  111.8 168.2 %reduce-scatter.5.cloned.1.call-start = ((), (), s32[]{:S(2)}) async-start(), calls=%async_computation.6 | async-start | bytes 2228224 | tf_op jit(solution)/shard_map/reduce_scatter | solution.py:252
  112.0 12.0 %copy-start.10 = (s32[8]{0:T(128)S(1)}, s32[8]{0:T(128)}, u32[]{:S(2)}) copy-start(s32[8]{0:T(128)} %copy-done.9) | copy-start | bytes 100
  112.0 12.0 %copy-start.11 = (s32[8]{0:T(128)S(1)}, s32[8]{0:T(128)}, u32[]{:S(2)}) copy-start(s32[8]{0:T(128)} %get-tuple-element.3) | copy-start | bytes 100
  112.0 12.0 %copy-start.7 = (pred[8]{0:T(512)(128)(4,1)S(1)}, pred[8]{0:T(512)(128)(4,1)}, u32[]{:S(2)}) copy-start(pred[8]{0:T(512)(128)(4,1)} %copy-done.6) | copy-start | bytes 28
  112.0 12.2 %copy-start.8 = (s32[32]{0:T(128)S(1)}, s32[32]{0:T(128)}, u32[]{:S(2)}) copy-start(s32[32]{0:T(128)} %get-tuple-element.5) | copy-start | bytes 388
  126.8 6.8 %copy-start.13 = (f32[64]{0:T(128)S(1)}, f32[64]{0:T(128)}, u32[]{:S(2)}) copy-start(f32[64]{0:T(128)} %negate_power_fusion) | copy-start | bytes 772
  126.8 6.6 %collective-permute-start.2 = (bf16[128,128]{0,1:T(8,128)(2,1)S(1)}, bf16[128,128]{0,1:T(8,128)(2,1)S(1)}, u32[]{:S(2)}, u32[]{:S(2)}) collective-permute-start(bf16[128,128]{0,1:T(8,128)(2,1)S(1)} %convolution_convert_fusion.4), channel_id=1, source_target_pairs={{0,1},{1,0},{2,3},{3,2},{4,5},{5,4},{6,7},{7,6},{8,9},{9,8},{10,11... | collective-permute-start | bytes 98312 | tf_op jit(solution)/shard_map/ppermute | solution.py:20
  134.6 5.3 %collective-permute-start.1 = (bf16[2,32,4,128]{3,2,0,1:T(4,128)(2,1)S(1)}, bf16[2,32,4,128]{3,2,0,1:T(4,128)(2,1)S(1)}, u32[]{:S(2)}, u32[]{:S(2)}) collective-permute-start(bf16[2,32,4,128]{3,2,0,1:T(4,128)(2,1)S(1)} %bitcast.187), channel_id=1, source_target_pairs={{0,1},{1,0},{2,3},{3,2},{4,5},{5,4},{6,7},{7,6},{8,9},{9,8},{10,11... | collective-permute-start | bytes 196616 | tf_op jit(solution)/shard_map/ppermute | solution.py:20
  192.8 12.2 %slice-start.2 = ((s8[8388608]{0:T(1024)(128)(4,1)}), s8[4194304]{0:T(1024)(128)(4,1)S(1)}, s32[]{:S(2)}) async-start(s8[8388608]{0:T(1024)(128)(4,1)} %bitcast.165), calls=%async_computation.9 | async-start | bytes 8388608
  196.8 8.2 %slice-start.3 = ((s8[8388608]{0:T(1024)(128)(4,1)}), s8[4194304]{0:T(1024)(128)(4,1)S(1)}, s32[]{:S(2)}) async-start(s8[8388608]{0:T(1024)(128)(4,1)} %bitcast.165), calls=%async_computation.10 | async-start | bytes 8388608
  200.6 4.3 %collective-permute-start.3 = (bf16[2,32,4,128]{3,1,2,0:T(8,128)(2,1)S(1)}, bf16[2,32,4,128]{3,1,2,0:T(8,128)(2,1)S(1)}, u32[]{:S(2)}, u32[]{:S(2)}) collective-permute-start(bf16[2,32,4,128]{3,1,2,0:T(8,128)(2,1)S(1)} %get-tuple-element.19), channel_id=1, source_target_pairs={{0,1},{1,0},{2,3},{3,2},{4,5},{5,4},{6,7},{7,6},{8,9},{9,8},{10,11... | collective-permute-start | bytes 196616 | tf_op jit(solution)/shard_map/ppermute | solution.py:20
  (5 other events, 6.1 us)
Sparse Core Ops, SparseCore 0:
  10.1 60.2 all-gather.2
  72.5 47.0 all-gather.4
  123.5 77.0 reduce-scatter.2
  207.9 72.1 reduce-scatter.4
where the time goes:
time: 287 us
  waiting for transfers between devices  166 us (58%)
  matrix products  47 us (16%)
  local copies, waits for them, and re-layouts  26.1 us (9%)
  other arithmetic  20.4 us (7%)
  between operations  17 us (6%)
  starting transfers between devices  10.2 us (4%)
    reduce_scatter x1, waiting for transfers between devices, body(): lax.psum_scatter(dec_terms.astype(jnp.bfloat16), 'tp', scatter_dimension=...  72.3 us
    all_to_all x1, waiting for transfers between devices, body(): lax.all_to_all(outgoing, 'grp', split_axis=0, concat_axis=0, tiled=True)  44.3 us
    all_gather x1, waiting for transfers between devices, body(): lax.all_gather(prefill_x, 'tp', axis=1, tiled=True)  39.1 us
    dot_general x2, matrix products, accumulate(): jnp.dot(piece, w_query, preferred_element_type=jnp.float32)  13.1 us
    gather x1, local copies, waits for them, and re-layouts, body(): cached = pool[page_ids].reshape(dec_dev, MAX_PAGES * PAGE, 2 * HEAD_DIM)  12 us
    ppermute x4, waiting for transfers between devices, from_partner(): return lax.ppermute(value, axis, pairs)  8.71 us
    dot_general x2, matrix products, accumulate(): jnp.dot(piece, w_keyval, preferred_element_type=jnp.float32)  6 us
  transfers between devices with their start and end apart: 9, of which 6 were waited for; matrix products, arithmetic and copies ran while one was open for 32% of the time, Pallas kernels for 0%

commit v1 on v0

v1 whole, which is shorter than its diff:
```python
import functools

import jax
import jax.numpy as jnp
from jax import lax
from jax.experimental import pallas as pl
from jax.experimental.pallas import tpu as pltpu
from jax.sharding import PartitionSpec as P

KV_HEADS = 8
HEAD_DIM = 128
SPANS = 8
PAGE = 16
MAX_PAGES = 32
RING = 4
BLOCKS = RING * RING
MESH = pl.DeviceIdType.MESH

rope_base = 500000.0
masked_score = -1e30


def place(dz, dx):
    return (dz % RING) * RING + dx % RING


def neighbours():
    me = lax.axis_index("tp")
    z = me // RING
    x = me % RING
    return {
        ("z", 1): ((z + 1) % RING) * RING + x,
        ("z", -1): ((z + RING - 1) % RING) * RING + x,
        ("x", 1): z * RING + (x + 1) % RING,
        ("x", -1): z * RING + (x + RING - 1) % RING,
    }


def greet(near):
    barrier = pltpu.get_barrier_semaphore()
    for device in near.values():
        pl.semaphore_signal(barrier, inc=1, device_id={"tp": device}, device_id_type=MESH)
    pl.semaphore_wait(barrier, len(near))


def absolute(dz, dx):
    me = lax.axis_index("tp")
    z = me // RING
    x = me % RING
    return ((z + dz) % RING) * RING + (x + dx) % RING


def axes_of(half, first):
    return ("x", "z") if (half == 0) == first else ("z", "x")


class Copies:
    def __init__(self, near, send, receive):
        self.near, self.send, self.receive = near, send, receive
        self.made = {}

    def start(self, name, axis, step, source, target):
        index = len(self.made)
        copy = pltpu.make_async_remote_copy(
            src_ref=source,
            dst_ref=target,
            send_sem=self.send.at[index],
            recv_sem=self.receive.at[index],
            device_id={"tp": self.near[axis, step]},
            device_id_type=MESH,
        )
        copy.start()
        self.made[name] = copy

    def arrive(self, name):
        self.made[name].wait_recv()

    def sent(self):
        for copy in self.made.values():
            copy.wait_send()


class Gather:
    def __init__(self, own, held, copies):
        self.own, self.held, self.copies = own, held, copies
        self.rows = own.shape[0]

    def slot(self, half, d1, d2):
        return place(d2, d1) if half == 0 else place(d1, d2)

    def part(self, half, d1, d2, quarter=None):
        count = self.rows // 2
        first = half * count
        if quarter is not None:
            count = count // 2
            first = first + quarter * count
        slot = self.slot(half, d1, d2)
        block = self.own if slot == 0 else self.held.at[slot]
        return block.at[pl.ds(first, count)]

    def first_sends(self):
        for half in (0, 1):
            axis = axes_of(half, True)[0]
            for step in (1, -1):
                self.copies.start(
                    ("1", half, step), axis, step, self.part(half, 0, 0), self.part(half, -step, 0)
                )
        self.second_sends(0)

    def second_sends(self, d1):
        for half in (0, 1):
            self.second_send(half, d1)

    def second_send(self, half, d1):
        axis = axes_of(half, True)[1]
        for step in (1, -1):
            self.copies.start(
                ("2", half, d1, step),
                axis,
                step,
                self.part(half, d1, 0),
                self.part(half, d1, -step),
            )

    def near_arrive(self):
        for half in (0, 1):
            axis = axes_of(half, True)[0]
            for step in (1, -1):
                quarter = 0 if step == 1 else 1
                self.copies.arrive(("1", half, step))
                self.copies.start(
                    ("1f", half, step),
                    axis,
                    step,
                    self.part(half, -step, 0, quarter),
                    self.part(half, -2 * step, 0, quarter),
                )
                self.second_send(half, -step)
        return [(half, d1, 0) for half in (0, 1) for d1 in (-1, 1)]

    def far_arrive(self):
        for half in (0, 1):
            for step in (1, -1):
                self.copies.arrive(("1f", half, step))
            self.second_send(half, 2)
        return [(half, 2, 0) for half in (0, 1)]

    def line_arrive(self, d1):
        for half in (0, 1):
            axis = axes_of(half, True)[1]
            for step in (1, -1):
                quarter = 0 if step == 1 else 1
                self.copies.arrive(("2", half, d1, step))
                self.copies.start(
                    ("2f", half, d1, step),
                    axis,
                    step,
                    self.part(half, d1, -step, quarter),
                    self.part(half, d1, -2 * step, quarter),
                )
        return [(half, d1, d2) for half in (0, 1) for d2 in (-1, 1)]

    def last_arrive(self, d1):
        for half in (0, 1):
            for step in (1, -1):
                self.copies.arrive(("2f", half, d1, step))
        return [(half, d1, 2) for half in (0, 1)]


class Scatter:
    def __init__(self, terms, relays, halves, relay2, halves2, out, copies):
        self.terms, self.relays, self.halves = terms, relays, halves
        self.relay2, self.halves2, self.out, self.copies = relay2, halves2, out, copies
        self.rows = terms.shape[1]

    def part(self, half, df, ds, quarter=None):
        count = self.rows // 2
        first = half * count
        if quarter is not None:
            count = count // 2
            first = first + quarter * count
        slot = place(df, ds) if half == 0 else place(ds, df)
        return self.terms.at[slot, pl.ds(first, count)]

    def relay_send(self, ds):
        for half in (0, 1):
            axis = axes_of(half, False)[0]
            for quarter, step in ((0, 1), (1, -1)):
                self.copies.start(
                    ("1r", half, ds, step),
                    axis,
                    step,
                    self.part(half, 2, ds, quarter),
                    self.relays.at[half, ds % RING, quarter],
                )

    def near_send(self, ds):
        for half in (0, 1):
            axis = axes_of(half, False)[0]
            for quarter, step in ((0, 1), (1, -1)):
                self.copies.arrive(("1r", half, ds, step))
                own = self.part(half, step, ds, quarter)
                added = self.relays[half, ds % RING, quarter].astype(jnp.float32)
                own[...] = (own[...].astype(jnp.float32) + added).astype(jnp.bfloat16)
                self.copies.start(
                    ("1", half, ds, step),
                    axis,
                    step,
                    self.part(half, step, ds),
                    self.halves.at[half, ds % RING, quarter],
                )

    def line_sum(self, ds):
        for half in (0, 1):
            for step in (1, -1):
                self.copies.arrive(("1", half, ds, step))
            own = self.part(half, 0, ds)
            total = own[...].astype(jnp.float32)
            for side in (0, 1):
                total = total + self.halves[half, ds % RING, side].astype(jnp.float32)
            own[...] = total.astype(jnp.bfloat16)

    def relay_send2(self):
        for half in (0, 1):
            axis = axes_of(half, False)[1]
            for quarter, step in ((0, 1), (1, -1)):
                self.copies.start(
                    ("2r", half, step),
                    axis,
                    step,
                    self.part(half, 0, 2, quarter),
                    self.relay2.at[half, quarter],
                )

    def near_send2(self):
        for half in (0, 1):
            axis = axes_of(half, False)[1]
            for quarter, step in ((0, 1), (1, -1)):
                self.copies.arrive(("2r", half, step))
                own = self.part(half, 0, step, quarter)
                added = self.relay2[half, quarter].astype(jnp.float32)
                own[...] = (own[...].astype(jnp.float32) + added).astype(jnp.bfloat16)
                self.copies.start(
                    ("2", half, step),
                    axis,
                    step,
                    self.part(half, 0, step),
                    self.halves2.at[half, quarter],
                )

    def finish(self):
        count = self.rows // 2
        for half in (0, 1):
            for step in (1, -1):
                self.copies.arrive(("2", half, step))
            total = self.part(half, 0, 0)[...].astype(jnp.float32)
            for side in (0, 1):
                total = total + self.halves2[half, side].astype(jnp.float32)
            self.out[pl.ds(half * count, count)] = total.astype(jnp.bfloat16)


def project_kernel(
    pre_x, dec_x, w_query, w_keyval, pre_out, dec_out, pre_held, dec_held, weights, load, send, receive
):
    near = neighbours()
    depth, wide = pre_x.shape[1], w_query.shape[1]
    loads = []
    for slot in range(BLOCKS):
        origin = absolute(slot // RING, slot % RING)
        rows = pl.ds(pl.multiple_of(origin * depth, depth), depth)
        loads.append(
            (
                pltpu.make_async_copy(
                    w_query.at[rows], weights.at[slot, :, pl.ds(0, wide)], load.at[0, slot]
                ),
                pltpu.make_async_copy(
                    w_keyval.at[rows],
                    weights.at[slot, :, pl.ds(wide, w_keyval.shape[1])],
                    load.at[1, slot],
                ),
            )
        )
    order = [place(*d) for d in ((0, 0), (0, -1), (0, 1), (-1, 0), (1, 0), (0, 2), (2, 0))]
    order = order + [slot for slot in range(BLOCKS) if slot not in order]
    for slot in order:
        for copy in loads[slot]:
            copy.start()
    greet(near)
    loaded = set()

    def multiply(gather, total, parts):
        for half, d1, d2 in parts:
            slot = gather.slot(half, d1, d2)
            if slot not in loaded:
                loaded.add(slot)
                for copy in loads[slot]:
                    copy.wait()
            count = gather.rows // 2
            rows = pl.ds(half * count, count)
            product = jnp.dot(
                gather.part(half, d1, d2)[...], weights[slot], preferred_element_type=jnp.float32
            )
            if slot == 0:
                total[rows] = product
            else:
                total[rows] += product

    pre = Gather(pre_x, pre_held, Copies(near, send.at[0], receive.at[0]))
    dec = Gather(dec_x, dec_held, Copies(near, send.at[1], receive.at[1]))
    pre.first_sends()
    multiply(pre, pre_out, [(0, 0, 0), (1, 0, 0)])
    multiply(pre, pre_out, pre.near_arrive())
    multiply(pre, pre_out, pre.far_arrive())
    for d1 in (0, -1, 1, 2):
        parts = pre.line_arrive(d1)
        if d1 == 2:
            dec.first_sends()
        multiply(pre, pre_out, parts)
    multiply(dec, dec_out, [(0, 0, 0), (1, 0, 0)])
    for d1 in (0, -1, 1, 2):
        multiply(pre, pre_out, pre.last_arrive(d1))
    multiply(dec, dec_out, dec.near_arrive())
    multiply(dec, dec_out, dec.far_arrive())
    for d1 in (0, -1, 1, 2):
        multiply(dec, dec_out, dec.line_arrive(d1))
    for d1 in (0, -1, 1, 2):
        multiply(dec, dec_out, dec.last_arrive(d1))
    pre.copies.sent()
    dec.copies.sent()


def project(pre_x, dec_x, w_query, w_keyval):
    wide = w_query.shape[1] + w_keyval.shape[1]
    depth = pre_x.shape[1]
    vmem = pl.BlockSpec(memory_space=pltpu.VMEM)
    hbm = pl.BlockSpec(memory_space=pl.ANY)
    return pl.pallas_call(
        project_kernel,
        out_shape=(
            jax.ShapeDtypeStruct((pre_x.shape[0], wide), jnp.float32),
            jax.ShapeDtypeStruct((dec_x.shape[0], wide), jnp.float32),
        ),
        in_specs=[vmem, vmem, hbm, hbm],
        out_specs=(vmem, vmem),
        scratch_shapes=[
            pltpu.VMEM((BLOCKS,) + pre_x.shape, jnp.bfloat16),
            pltpu.VMEM((BLOCKS,) + dec_x.shape, jnp.bfloat16),
            pltpu.VMEM((BLOCKS, depth, wide), jnp.bfloat16),
            pltpu.SemaphoreType.DMA((2, BLOCKS)),
            pltpu.SemaphoreType.DMA((2, 40)),
            pltpu.SemaphoreType.DMA((2, 40)),
        ],
        compiler_params=pltpu.CompilerParams(
            collective_id=0, has_side_effects=True, vmem_limit_bytes=48 * 2**20
        ),
        name="gather_project",
    )(pre_x, dec_x, w_query, w_keyval)


ORDER = (
    ((2, 2),),
    ((2, -1), (-1, 2)),
    ((2, 1), (1, 2)),
    ((2, 0), (0, 2)),
    ((-1, -1), (-1, 1), (1, -1), (1, 1)),
    ((-1, 0), (1, 0), (0, -1), (0, 1)),
    ((0, 0),),
)


def output_kernel(
    pre_heads,
    dec_heads,
    w_out,
    pre_out,
    dec_out,
    weights,
    pre_terms,
    pre_relays,
    pre_halves,
    pre_relay2,
    pre_halves2,
    dec_terms,
    dec_relays,
    dec_halves,
    dec_relay2,
    dec_halves2,
    load,
    send,
    receive,
):
    near = neighbours()
    width = pre_out.shape[1]
    loads = {}
    for blocks in ORDER:
        for dz, dx in blocks:
            slot = place(dz, dx)
            columns = pl.ds(pl.multiple_of(absolute(dz, dx) * width, width), width)
            loads[slot] = pltpu.make_async_copy(
                w_out.at[:, columns], weights.at[slot], load.at[slot]
            )
            loads[slot].start()
    greet(near)
    loaded = set()

    def terms(heads, kept, blocks):
        for dz, dx in blocks:
            slot = place(dz, dx)
            if slot not in loaded:
                loaded.add(slot)
                loads[slot].wait()
            kept[slot] = jnp.dot(
                heads[...], weights[slot], preferred_element_type=jnp.float32
            ).astype(jnp.bfloat16)

    pre = Scatter(
        pre_terms, pre_relays, pre_halves, pre_relay2, pre_halves2, pre_out,
        Copies(near, send.at[0], receive.at[0]),
    )
    dec = Scatter(
        dec_terms, dec_relays, dec_halves, dec_relay2, dec_halves2, dec_out,
        Copies(near, send.at[1], receive.at[1]),
    )
    for scatter, heads, kept in ((pre, pre_heads, pre_terms), (dec, dec_heads, dec_terms)):
        for index, ds in enumerate((2, -1, 1, 0)):
            terms(heads, kept, ORDER[index])
            scatter.relay_send(ds)
        scatter.near_send(2)
        terms(heads, kept, ORDER[4])
        scatter.near_send(-1)
        scatter.near_send(1)
        terms(heads, kept, ORDER[5])
        scatter.near_send(0)
        terms(heads, kept, ORDER[6])
    for scatter in (pre, dec):
        scatter.line_sum(2)
        scatter.relay_send2()
        scatter.line_sum(-1)
        scatter.line_sum(1)
        scatter.near_send2()
        scatter.line_sum(0)
        scatter.finish()
    pre.copies.sent()
    dec.copies.sent()


def scatter_scratch(rows, width):
    half, quarter = rows // 2, rows // 4
    return [
        pltpu.VMEM((BLOCKS, rows, width), jnp.bfloat16),
        pltpu.VMEM((2, RING, 2, quarter, width), jnp.bfloat16),
        pltpu.VMEM((2, RING, 2, half, width), jnp.bfloat16),
        pltpu.VMEM((2, 2, quarter, width), jnp.bfloat16),
        pltpu.VMEM((2, 2, half, width), jnp.bfloat16),
    ]


def output(pre_heads, dec_heads, w_out):
    width = w_out.shape[1] // BLOCKS
    vmem = pl.BlockSpec(memory_space=pltpu.VMEM)
    hbm = pl.BlockSpec(memory_space=pl.ANY)
    return pl.pallas_call(
        output_kernel,
        out_shape=(
            jax.ShapeDtypeStruct((pre_heads.shape[0], width), jnp.bfloat16),
            jax.ShapeDtypeStruct((dec_heads.shape[0], width), jnp.bfloat16),
        ),
        in_specs=[vmem, vmem, hbm],
        out_specs=(vmem, vmem),
        scratch_shapes=[pltpu.VMEM((BLOCKS, w_out.shape[0], width), jnp.bfloat16)]
        + scatter_scratch(pre_heads.shape[0], width)
        + scatter_scratch(dec_heads.shape[0], width)
        + [
            pltpu.SemaphoreType.DMA((BLOCKS,)),
            pltpu.SemaphoreType.DMA((2, 40)),
            pltpu.SemaphoreType.DMA((2, 40)),
        ],
        compiler_params=pltpu.CompilerParams(
            collective_id=1, has_side_effects=True, vmem_limit_bytes=48 * 2**20
        ),
        name="project_scatter",
    )(pre_heads, dec_heads, w_out)


def from_partner(value, axis, distance):
    mask = 2**distance
    pairs = [(source, source ^ mask) for source in range(lax.axis_size(axis))]
    return lax.ppermute(value, axis, pairs)


def rotary(values, positions):
    half = values.shape[-1] // 2
    exponent = jnp.arange(half, dtype=jnp.float32) * (2.0 / values.shape[-1])
    angles = positions.astype(jnp.float32)[..., None] * rope_base ** (-exponent)
    cosine = jnp.cos(angles)
    sine = jnp.sin(angles)
    first = values[..., :half]
    second = values[..., half:]
    return jnp.concatenate([first * cosine - second * sine, second * cosine + first * sine], -1)


def ordered(mine, theirs, member, axis):
    return jnp.where(
        member == 0, jnp.concatenate([mine, theirs], axis), jnp.concatenate([theirs, mine], axis)
    )


def joined_softmax(first, second):
    highest = jnp.maximum(jnp.max(first, -1), jnp.max(second, -1))[..., None]
    first = jnp.exp(first - highest)
    second = jnp.exp(second - highest)
    totals = (jnp.sum(first, -1) + jnp.sum(second, -1))[..., None]
    return (first / totals).astype(jnp.bfloat16), (second / totals).astype(jnp.bfloat16)


def einsum(form, left, right):
    return jnp.einsum(form, left, right, preferred_element_type=jnp.float32)


def body(
    prefill_x,
    span_index,
    prefix_pages,
    prefix_cache,
    decode_x,
    decode_len,
    page_order,
    assignment,
    kv_cache,
    w_query,
    w_keyval,
    w_out,
):
    split = lax.axis_size("tp") // KV_HEADS
    member = lax.axis_index("tp") % split
    group = lax.axis_index("grp")
    prompts = lax.axis_size("grp")
    span = prefill_x.shape[0]
    decode = decode_x.shape[1]
    rows = 2 * decode
    dec_dev = decode // split
    query_wide = w_query.shape[1]
    heads_dev = query_wide // HEAD_DIM
    pre_rows = prefix_cache.shape[2]
    context_rows = pre_rows + span
    scale = HEAD_DIM ** (-0.5)

    pre_all, dec_all = project(
        prefill_x, decode_x.reshape(rows, decode_x.shape[2]), w_query, w_keyval
    )
    pre_query, pre_half = pre_all[:, :query_wide], pre_all[:, query_wide:].astype(jnp.bfloat16)
    dec_query, dec_half = dec_all[:, :query_wide], dec_all[:, query_wide:].astype(jnp.bfloat16)
    halves = jnp.concatenate([pre_half, dec_half], 0)
    whole = ordered(halves, from_partner(halves, "tp", 0), member, 1)
    pre_whole, dec_whole = whole[:span], whole[span:]

    start_row = span_index[group] * span
    pre_spots = start_row + jnp.arange(span, dtype=jnp.int32)
    queries = rotary(pre_query.reshape(span, heads_dev, HEAD_DIM), pre_spots[:, None]).astype(
        jnp.bfloat16
    )
    pre_keys = rotary(pre_whole[:, :HEAD_DIM].astype(jnp.float32), pre_spots).astype(jnp.bfloat16)
    pre_values = pre_whole[:, HEAD_DIM:]
    prior = prefix_cache.reshape(pre_rows, 2 * HEAD_DIM)
    pages = pre_rows // PAGE
    page_live = jnp.any(
        (prefix_pages[0][:, None] == jnp.arange(pages, dtype=jnp.int32)[None, :])
        & (jnp.arange(pages, dtype=jnp.int32)[:, None] < start_row // PAGE),
        0,
    )
    prior_live = jnp.repeat(page_live, PAGE)
    prior_scores = einsum("qhd,kd->hqk", queries, prior[:, :HEAD_DIM]) * scale
    prior_scores = jnp.where(prior_live[None, None, :], prior_scores, masked_score)
    own_scores = einsum("qhd,kd->hqk", queries, pre_keys) * scale
    causal = jnp.arange(span)[:, None] >= jnp.arange(span)[None, :]
    own_scores = jnp.where(causal[None], own_scores, masked_score)
    prior_weights, own_weights = joined_softmax(prior_scores, own_scores)
    pre_heads = einsum("hqk,kd->qhd", prior_weights, prior[:, HEAD_DIM:])
    pre_heads = pre_heads + einsum("hqk,kd->qhd", own_weights, pre_values)
    pre_heads = pre_heads.astype(jnp.bfloat16).reshape(span, heads_dev * HEAD_DIM)

    finished = span_index == SPANS - 1
    sources = jnp.arange(prompts, dtype=jnp.int32)
    to_here = (assignment == group) & finished
    ranks = jnp.sum(to_here[None, :] & (sources[None, :] < sources[:, None]), 1)
    owner = ranks % split * dec_dev + ranks // split
    all_lengths = decode_len.reshape(decode)
    sequence_ids = jnp.arange(decode, dtype=jnp.int32)
    owned = (owner[:, None] == sequence_ids[None, :]) & to_here[:, None]
    has_context = jnp.any(owned, 0)
    base = jnp.where(has_context, context_rows, all_lengths)
    spots = base[None, :] + jnp.arange(2, dtype=jnp.int32)[:, None]
    dec_queries = rotary(
        dec_query.reshape(2, decode, heads_dev, HEAD_DIM), spots[:, :, None]
    ).astype(jnp.bfloat16)
    new_keys = rotary(
        dec_whole[:, :HEAD_DIM].astype(jnp.float32).reshape(2, decode, HEAD_DIM), spots
    ).astype(jnp.bfloat16)
    new_values = dec_whole[:, HEAD_DIM:].reshape(2, decode, HEAD_DIM)
    step_order = jnp.arange(2)[:, None] >= jnp.arange(2)[None, :]

    picks = owned.astype(jnp.bfloat16)
    steps = jnp.concatenate(
        [dec_queries.reshape(2, decode, query_wide), new_keys, new_values], -1
    )
    visiting = einsum("sj,tjc->stc", picks, steps).astype(jnp.bfloat16)
    visiting = lax.all_to_all(visiting, "grp", split_axis=0, concat_axis=0, tiled=True)
    visiting = jnp.sum(visiting.astype(jnp.float32), 0).astype(jnp.bfloat16)
    visit_queries = visiting[:, :query_wide].reshape(2, heads_dev, HEAD_DIM)
    visit_keys = visiting[:, query_wide : query_wide + HEAD_DIM]
    visit_values = visiting[:, query_wide + HEAD_DIM :]
    context = jnp.concatenate([prior, jnp.concatenate([pre_keys, pre_values], 1)], 0)
    context_scores = einsum("tgd,cd->tgc", visit_queries, context[:, :HEAD_DIM]) * scale
    step_scores = einsum("tgd,ud->tgu", visit_queries, visit_keys) * scale
    step_scores = jnp.where(step_order[:, None, :], step_scores, masked_score)
    context_weights, step_weights = joined_softmax(context_scores, step_scores)
    taken = einsum("tgc,cd->tgd", context_weights, context[:, HEAD_DIM:])
    taken = taken + einsum("tgu,ud->tgd", step_weights, visit_values)
    taken = lax.all_gather(taken.astype(jnp.bfloat16), "grp")

    block_queries = dec_queries.reshape(2, split, dec_dev, heads_dev, HEAD_DIM)
    mine = lax.dynamic_index_in_dim(block_queries, member, 1, keepdims=False)
    others = lax.dynamic_index_in_dim(block_queries, 1 - member, 1, keepdims=False)
    group_queries = ordered(mine, from_partner(others, "tp", 0), member, 2)
    my_keys = lax.dynamic_index_in_dim(
        new_keys.reshape(2, split, dec_dev, HEAD_DIM), member, 1, keepdims=False
    )
    my_values = lax.dynamic_index_in_dim(
        new_values.reshape(2, split, dec_dev, HEAD_DIM), member, 1, keepdims=False
    )
    my_lengths = lax.dynamic_index_in_dim(decode_len[0], member, 0, keepdims=False)
    my_order = lax.dynamic_index_in_dim(page_order[0], member, 0, keepdims=False)
    pool_dev = my_order.shape[0]
    counts = (my_lengths + PAGE - 1) // PAGE
    firsts = jnp.cumsum(counts) - counts
    slots = jnp.clip(
        firsts[:, None] + jnp.arange(MAX_PAGES, dtype=jnp.int32)[None, :], 0, pool_dev - 1
    )
    page_ids = my_order[slots]
    pool = kv_cache.reshape(pool_dev, PAGE, 2 * HEAD_DIM)
    cached = pool[page_ids].reshape(dec_dev, MAX_PAGES * PAGE, 2 * HEAD_DIM)
    live = jnp.arange(MAX_PAGES * PAGE)[None, :] < my_lengths[:, None]
    pool_scores = einsum("tjgd,jcd->jtgc", group_queries, cached[..., :HEAD_DIM]) * scale
    pool_scores = jnp.where(live[:, None, None, :], pool_scores, masked_score)
    fresh_scores = einsum("tjgd,ujd->jtgu", group_queries, my_keys) * scale
    fresh_scores = jnp.where(step_order[None, :, None, :], fresh_scores, masked_score)
    pool_weights, fresh_weights = joined_softmax(pool_scores, fresh_scores)
    attended = einsum("jtgc,jcd->tjgd", pool_weights, cached[..., HEAD_DIM:])
    attended = attended + einsum("jtgu,ujd->tjgd", fresh_weights, my_values)
    attended = attended.astype(jnp.bfloat16)
    keep_heads = lax.dynamic_slice_in_dim(attended, member * heads_dev, heads_dev, 2)
    away_heads = lax.dynamic_slice_in_dim(attended, (1 - member) * heads_dev, heads_dev, 2)
    own_heads = ordered(keep_heads, from_partner(away_heads, "tp", 0), member, 1)
    placed = einsum("sj,stgd->tjgd", picks, taken).astype(jnp.bfloat16)
    own_heads = jnp.where(has_context[None, :, None, None], placed, own_heads)

    prefill_out, decode_out = output(pre_heads, own_heads.reshape(rows, query_wide), w_out)
    return (prefill_out, decode_out.reshape(2, decode, -1))


def solution(mesh):
    placed = (
        P("grp", "tp"),
        P(),
        P("grp", None),
        P("grp", "tp", None, None),
        P(None, "grp", "tp"),
        P("grp", None, None),
        P("grp", None, None),
        P(),
        P("grp", "tp", None, None),
        P(None, "tp"),
        P(None, "tp"),
        P("tp", None),
    )
    return jax.shard_map(
        body,
        mesh=mesh,
        in_specs=placed,
        out_specs=(P("grp", "tp"), P(None, "grp", "tp")),
        check_vma=False,
    )
```

time: 287 us -> 160 us (0.56)
  waiting for transfers between devices: 166 us -> 0.01 us
  Pallas kernels: 0 us -> 93.8 us
  matrix products: 47 us -> 13.3 us
  between operations: 17 us -> 1.82 us
  other arithmetic: 20.4 us -> 5.7 us
  blocking collectives: 0 us -> 12.6 us
    pallas_call x0 -> x2, Pallas kernels: none -> 93.8 us  [the longest x1 48.2 us: project(): pl.pallas_call(project_kernel, out_shape=(jax.ShapeDtypeStruct((pre_x.sha...]
    reduce_scatter x2 -> x0, waiting for transfers between devices: 72.3 us -> none  [the longest x1 72.3 us: body(): lax.psum_scatter(dec_terms.astype(jnp.bfloat16), 'tp', scatter_dimension=...]
    all_to_all x1, waiting for transfers between devices: 44.3 us -> 0.01 us  [body(): lax.all_to_all(visiting, 'grp', split_axis=0, concat_axis=0, tiled=True)]
    all_gather x2 -> x0, waiting for transfers between devices: 39.1 us -> none  [the longest x1 39.1 us: body(): lax.all_gather(prefill_x, 'tp', axis=1, tiled=True)]
    dot_general x22 -> x14, matrix products: 47 us -> 13.3 us  [einsum(): return jnp.einsum(form, left, right, preferred_element_type=jnp.float32)]
    all_gather x0 -> x1, blocking collectives: none -> 12.6 us  [body(): taken = lax.all_gather(taken.astype(jnp.bfloat16), 'grp')]
    ppermute x4 -> x3, waiting for transfers between devices: 8.71 us -> 0.01 us  [from_partner(): return lax.ppermute(value, axis, pairs)]
    select_n x3 -> x1, other arithmetic: 4.48 us -> 0.01 us  [body(): base = jnp.where(has_context, context_rows, all_lengths)]
  transfers between devices with their start and end apart: 9 -> 4, of which waited for: 6 -> 0; matrix products, arithmetic and copies ran while one was open for 32% -> 18% of each run, Pallas kernels for 0% -> 0%
where the time goes in v1:
time: 160 us
  Pallas kernels  93.8 us (59%)
  local copies, waits for them, and re-layouts  24.3 us (15%)
  matrix products  13.3 us (8%)
  blocking collectives  12.6 us (8%)
  starting transfers between devices  8.05 us (5%)
  other arithmetic  5.7 us (4%)
  between operations  1.82 us (1%)
    pallas_call x1, Pallas kernels, project(): pl.pallas_call(project_kernel, out_shape=(jax.ShapeDtypeStruct((pre_x.sha...  48.2 us
    pallas_call x1, Pallas kernels, output(): pl.pallas_call(output_kernel, out_shape=(jax.ShapeDtypeStruct((pre_heads....  45.6 us
    dot_general x14, matrix products, einsum(): return jnp.einsum(form, left, right, preferred_element_type=jnp.float32)  13.3 us
    all_gather x1, blocking collectives, body(): taken = lax.all_gather(taken.astype(jnp.bfloat16), 'grp')  12.6 us
    gather x1, local copies, waits for them, and re-layouts, body(): cached = pool[page_ids].reshape(dec_dev, MAX_PAGES * PAGE, 2 * HEAD_DIM)  12 us
    unnamed x23, local copies, waits for them, and re-layouts  4.91 us
    gather x2, local copies, waits for them, and re-layouts, body(): page_ids = my_order[slots]  4.6 us
    all_to_all x1, starting transfers between devices, body(): lax.all_to_all(visiting, 'grp', split_axis=0, concat_axis=0, tiled=True)  4.47 us
  transfers between devices with their start and end apart: 4, of which 0 were waited for; matrix products, arithmetic and copies ran while one was open for 18% of the time, Pallas kernels for 0%

profile of v1, /device:TPU:0, one launch (start us, length us, event | category | flops | bytes accessed | tf_op | source)
XLA Modules:
  0.0 159.6 jit_solution(18146986888036565866)
XLA Ops:
  0.7 1.6 copy-done.1
  2.3 0.9 copy-done.2
  3.2 0.9 copy-done.3
  4.1 48.2 %gather_project.1 = (f32[256,640]{1,0:T(8,128)S(1)}, f32[128,640]{1,0:T(8,128)S(1)}) custom-call(bf16[256,512]{1,0:T(8,128)(2,1)S(1)} %copy-done.2, bf16[128,512]{1,0:T(8,128)(2,1)S(1)} %bitcast.148, bf16[8192,512]{1,0:T(8,128)(2,1)} %w_query.1, bf16[8192,128]{1,0:T(8,128)(2,1)S(1)} %copy-done.1), custom_call_target="tpu_custom_call" | custom-call | tf_op jit(solution)/shard_map/gather_project/pallas_call | solution.py:337
  52.3 1.4 collective-permute-start
  53.7 0.6 dynamic_slice.31
  56.3 4.5 %gather_fusion = s32[1024]{0:T(1024)S(1)} fusion(s32[544]{0:T(1024)S(1)} %fusion.60, s32[1024]{0:T(1024)S(1)} %broadcast_clamp_fusion), kind=kCustom, calls=%fused_computation | custom fusion | bytes 12288 | tf_op jit(solution)/shard_map/gather | solution.py:639
  61.8 12.0 %gather_fusion.1 = bf16[1024,16,256]{2,1,0:T(8,128)(2,1)} fusion(bf16[544,16,256]{2,1,0:T(8,128)(2,1)} %bitcast.150, s32[1024]{0:T(1024)S(1)} %broadcast_clamp_fusion.1), kind=kCustom, calls=%fused_computation.1 | custom fusion | bytes 16781312 | tf_op jit(solution)/shard_map/gather | solution.py:641
  75.0 0.8 collective-permute-start.1
  76.1 0.6 copy.82
  76.7 4.5 %all-to-all-start = ((bf16[8,2,768]{2,1,0:T(2,128)(2,1)}), bf16[8,2,768]{2,1,0:T(2,128)(2,1)S(1)}, u32[]{:S(2)}, u32[]{:S(2)}) async-start(bf16[8,2,768]{2,1,0:T(2,128)(2,1)} %copy.82), calls=%async_computation | async-start | bytes 49152 | tf_op jit(solution)/shard_map/all_to_all | solution.py:607
  81.2 0.6 subtract_convert_fusion.2
  82.1 0.4 fusion.84
  82.5 1.4 bitcast_reduce_fusion
  84.1 1.7 %fusion.1 = f32[4,256]{1,0:T(4,128)S(1)} fusion(f32[256,4,1792]{2,0,1:T(8,128)S(1)} %get-tuple-element.35, f32[4,256]{1,0:T(4,128)S(1)} %max.27, pred[1792]{0:T(1024)(128)(4,1)S(1)} %broadcast_in_dim.66), kind=kLoop, calls=%fused_computation.7 | loop fusion | flops 7339008 | bytes 7350016 | tf_op jit(solution)/shard_map/reduce_sum | solution.py:512
  85.8 2.2 %fusion.10 = f32[256,4,128]{0,2,1:T(8,128)S(1)} fusion(f32[256,4,1792]{2,0,1:T(8,128)S(1)} %get-tuple-element.35, f32[4,256]{1,0:T(4,128)S(1)} %add.206, f32[4,256]{1,0:T(4,128)S(1)} %max.27, pred[1792]{0:T(1024)(128)(4,1)S(1)} %broadcast_in_dim.66, bf16[1792,256]{1,0:T(8,128)(2,1)S(1)} %bitcast.155), kind=kOutput, calls=%fused_computation.21 | convolution fusion | flops 478937088 | bytes 8333312 | tf_op jit(solution)/shard_map/hqk,kd->qhd/dot_general | solution.py:517
  89.8 0.7 fusion.86
  90.5 3.5 %fusion.85 = (f32[32,2,8]{2,1,0:T(2,128)S(1)}, f32[32,2,8,512]{3,2,1,0:T(8,128)S(1)}) fusion(bf16[32,512,256]{2,1,0:T(8,128)(2,1)} %bitcast.151, bf16[2,32,4,128]{3,2,0,1:T(4,128)(2,1)S(1)} %collective-permute-done.1, bf16[2,32,4,128]{3,2,0,1:T(4,128)(2,1)S(1)} %bitcast.167, pred[]{:T(512)S(6)} %eq.50, pred[32,512]{1,0:T(8,128)(4,1)S(1)} %iota_compare_fusion.1), kind=kOutput, calls=%fused_computation.181 | convolution fusion | flops 68484608 | bytes 5392385 | tf_op jit(solution)/shard_map/tjgd,jcd->jtgc/dot_general | solution.py:517
  94.5 3.0 %fusion.3 = f32[32,128,2,8]{1,3,2,0:T(8,128)S(1)} fusion(bf16[32,512,256]{2,1,0:T(8,128)(2,1)} %bitcast.152, f32[32,2,8,512]{3,2,1,0:T(8,128)S(1)} %get-tuple-element.39, f32[32,2,8]{2,1,0:T(2,128)S(1)} %add.224, f32[32,2,8]{2,1,0:T(2,128)S(1)} %max.30), kind=kOutput, calls=%fused_computation.11 | convolution fusion | flops 67895296 | bytes 5509120 | tf_op jit(solution)/shard_map/jtgc,jcd->tjgd/dot_general | solution.py:517
  98.0 1.4 collective-permute-start.2
  99.6 12.6 %all-gather = bf16[16,4,128]{2,1,0:T(4,128)(2,1)S(1)} all-gather(bf16[2,4,128]{2,1,0:T(4,128)(2,1)S(1)} %fusion.14), channel_id=2, replica_groups=mesh['grp'=8,'tp'=16] {'grp'}, dimensions={0}, use_global_device_ids=true | all-gather | bytes 18432 | tf_op jit(solution)/shard_map/all_gather | solution.py:619
  112.6 45.6 %project_scatter.1 = (bf16[256,512]{1,0:T(8,128)(2,1)S(1)}, bf16[128,512]{1,0:T(8,128)(2,1)S(1)}) custom-call(bf16[256,512]{1,0:T(8,128)(2,1)S(1)} %copy.103.pre_heads, bf16[128,512]{1,0:T(8,128)(2,1)S(1)} %bitcast.147, bf16[512,8192]{1,0:T(8,128)(2,1)} %w_out.1), custom_call_target="tpu_custom_call" | custom-call | tf_op jit(solution)/shard_map/project_scatter/pallas_call | solution.py:462
  158.2 0.7 copy.142
  159.0 0.7 copy.143
  (97 shorter events, 7.2 us)
Async XLA Ops:
  0.6 54.9 %copy-start = (s32[1,2,544]{2,1,0:T(2,128)S(1)}, s32[1,2,544]{2,1,0:T(2,128)}, u32[]{:S(2)}) copy-start(s32[1,2,544]{2,1,0:T(2,128)} %param.18) | copy-start | bytes 13060
  0.6 53.1 %copy-start.5 = (s32[8]{0:T(128)S(1)}, s32[8]{0:T(128)}, u32[]{:S(2)}) copy-start(s32[8]{0:T(128)} %param.13) | copy-start | bytes 100
  0.7 54.5 %copy-start.6 = (s32[8]{0:T(128)S(1)}, s32[8]{0:T(128)}, u32[]{:S(2)}) copy-start(s32[8]{0:T(128)} %param.19) | copy-start | bytes 100
  0.7 54.9 %copy-start.8 = (s32[1,112]{1,0:T(1,128)S(1)}, s32[1,112]{1,0:T(1,128)}, u32[]{:S(2)}) copy-start(s32[1,112]{1,0:T(1,128)} %param.14) | copy-start | bytes 1348
  0.7 1.6 %copy-start.1 = (bf16[8192,128]{1,0:T(8,128)(2,1)S(1)}, bf16[8192,128]{1,0:T(8,128)(2,1)}, u32[]{:S(2)}) copy-start(bf16[8192,128]{1,0:T(8,128)(2,1)} %w_keyval.1) | copy-start | bytes 6291460
  2.3 0.9 copy-start.2
  3.2 0.9 copy-start.3
  4.1 51.3 %copy-start.7 = (s32[1,2,32]{2,1,0:T(2,128)S(1)}, s32[1,2,32]{2,1,0:T(2,128)}, u32[]{:S(2)}) copy-start(s32[1,2,32]{2,1,0:T(2,128)} %param.17) | copy-start | bytes 772
  52.3 21.5 %collective-permute-start = (bf16[384,128]{1,0:T(8,128)(2,1)S(1)}, bf16[384,128]{1,0:T(8,128)(2,1)S(1)}, u32[]{:S(2)}, u32[]{:S(2)}) collective-permute-start(bf16[384,128]{1,0:T(8,128)(2,1)S(1)} %pad_maximum_fusion.2), channel_id=1, source_target_pairs={{0,1},{1,0},{2,3},{3,2},{4,5},{5,4},{6,7},{7,6},{8,9},{9,8},{10,11... | collective-permute-start | bytes 294920 | tf_op jit(solution)/shard_map/ppermute | solution.py:488
  61.8 20.2 %copy-start.4 = (bf16[1,1,1792,256]{3,2,1,0:T(8,128)(2,1)S(1)}, bf16[1,1,1792,256]{3,2,1,0:T(8,128)(2,1)}, u32[]{:S(2)}) copy-start(bf16[1,1,1792,256]{3,2,1,0:T(8,128)(2,1)} %param.15) | copy-start | bytes 2752516
  75.0 14.7 %collective-permute-start.1 = (bf16[2,32,4,128]{3,2,0,1:T(4,128)(2,1)S(1)}, bf16[2,32,4,128]{3,2,0,1:T(4,128)(2,1)S(1)}, u32[]{:S(2)}, u32[]{:S(2)}) collective-permute-start(bf16[2,32,4,128]{3,2,0,1:T(4,128)(2,1)S(1)} %bitcast.165), channel_id=1, source_target_pairs={{0,1},{1,0},{2,3},{3,2},{4,5},{5,4},{6,7},{7,6},{8,9},{9,8},{10,11... | collective-permute-start | bytes 196616 | tf_op jit(solution)/shard_map/ppermute | solution.py:488
  76.7 12.0 %all-to-all-start = ((bf16[8,2,768]{2,1,0:T(2,128)(2,1)}), bf16[8,2,768]{2,1,0:T(2,128)(2,1)S(1)}, u32[]{:S(2)}, u32[]{:S(2)}) async-start(bf16[8,2,768]{2,1,0:T(2,128)(2,1)} %copy.82), calls=%async_computation | async-start | bytes 49152 | tf_op jit(solution)/shard_map/all_to_all | solution.py:607
  98.0 14.2 %collective-permute-start.2 = (bf16[2,32,4,128]{3,1,2,0:T(8,128)(2,1)S(1)}, bf16[2,32,4,128]{3,1,2,0:T(8,128)(2,1)S(1)}, u32[]{:S(2)}, u32[]{:S(2)}) collective-permute-start(bf16[2,32,4,128]{3,1,2,0:T(8,128)(2,1)S(1)} %get-tuple-element.27), channel_id=1, source_target_pairs={{0,1},{1,0},{2,3},{3,2},{4,5},{5,4},{6,7},{7,6},{8,9},{9,8},{10,11... | collective-permute-start | bytes 196616 | tf_op jit(solution)/shard_map/ppermute | solution.py:488

commit v2 on v1

v2 whole, which is shorter than its diff:
```python
import functools
import types

import jax
import jax.numpy as jnp
import numpy as np
from jax import lax
from jax.experimental import pallas as pl
from jax.experimental.pallas import tpu as pltpu
from jax.sharding import PartitionSpec as P

KV_HEADS = 8
HEAD_DIM = 128
SPANS = 8
PAGE = 16
MAX_PAGES = 32
RING = 4
BLOCKS = RING * RING
SPLIT = 2
GROUPS = 8
STEP_ROWS = 16
MESH = pl.DeviceIdType.MESH

rope_base = 500000.0
masked_score = -1e30


def place(dz, dx):
    return (dz % RING) * RING + dx % RING


def neighbours():
    me = lax.axis_index("tp")
    z = me // RING
    x = me % RING
    return {
        ("z", 1): ((z + 1) % RING) * RING + x,
        ("z", -1): ((z + RING - 1) % RING) * RING + x,
        ("x", 1): z * RING + (x + 1) % RING,
        ("x", -1): z * RING + (x + RING - 1) % RING,
    }


def absolute(dz, dx):
    me = lax.axis_index("tp")
    z = me // RING
    x = me % RING
    return ((z + dz) % RING) * RING + (x + dx) % RING


def axes_of(half, first):
    return ("x", "z") if (half == 0) == first else ("z", "x")


def await_bytes(region, semaphore):
    pltpu.make_async_copy(region, region, semaphore).wait()


class Copies:
    def __init__(self, near, send, receive):
        self.near, self.send, self.receive = near, send, receive
        self.index = {}

    def start(self, name, axis, step, source, target):
        index = self.index.setdefault(name, len(self.index))
        pltpu.make_async_remote_copy(
            src_ref=source,
            dst_ref=target,
            send_sem=self.send,
            recv_sem=self.receive.at[index],
            device_id={"tp": self.near[axis, step]},
            device_id_type=MESH,
        ).start()

    def arrive(self, name, region):
        await_bytes(region, self.receive.at[self.index[name]])

    def sent(self, region):
        await_bytes(region, self.send)


class Gather:
    def __init__(self, own, held, copies):
        self.own, self.held, self.copies = own, held, copies
        self.rows = own.shape[0]

    def slot(self, half, d1, d2):
        return place(d2, d1) if half == 0 else place(d1, d2)

    def part(self, half, d1, d2, quarter=None):
        count = self.rows // 2
        first = half * count
        if quarter is not None:
            count = count // 2
            first = first + quarter * count
        return self.held.at[self.slot(half, d1, d2), pl.ds(first, count)]

    def mine(self, half):
        count = self.rows // 2
        return self.held.at[0, pl.ds(half * count, count)]

    def first_sends(self):
        for half in (0, 1):
            axis = axes_of(half, True)[0]
            for step in (1, -1):
                self.copies.start(
                    ("1", half, step), axis, step, self.mine(half), self.part(half, -step, 0)
                )
        self.second_sends(0)

    def second_sends(self, d1):
        for half in (0, 1):
            self.second_send(half, d1)

    def second_send(self, half, d1):
        axis = axes_of(half, True)[1]
        for step in (1, -1):
            self.copies.start(
                ("2", half, d1, step),
                axis,
                step,
                self.part(half, d1, 0) if d1 != 0 else self.mine(half),
                self.part(half, d1, -step),
            )

    def near_arrive(self):
        for half in (0, 1):
            axis = axes_of(half, True)[0]
            for step in (1, -1):
                quarter = 0 if step == 1 else 1
                self.copies.arrive(("1", half, step), self.part(half, -step, 0))
                self.copies.start(
                    ("1f", half),
                    axis,
                    step,
                    self.part(half, -step, 0, quarter),
                    self.part(half, -2 * step, 0, quarter),
                )
                self.second_send(half, -step)
        return [(half, d1, 0) for half in (0, 1) for d1 in (-1, 1)]

    def far_arrive(self):
        for half in (0, 1):
            self.copies.arrive(("1f", half), self.part(half, 2, 0))
            self.second_send(half, 2)
        return [(half, 2, 0) for half in (0, 1)]

    def line_arrive(self, d1):
        for half in (0, 1):
            axis = axes_of(half, True)[1]
            for step in (1, -1):
                quarter = 0 if step == 1 else 1
                self.copies.arrive(("2", half, d1, step), self.part(half, d1, -step))
                self.copies.start(
                    ("2f", half, d1),
                    axis,
                    step,
                    self.part(half, d1, -step, quarter),
                    self.part(half, d1, -2 * step, quarter),
                )
        return [(half, d1, d2) for half in (0, 1) for d2 in (-1, 1)]

    def last_arrive(self, d1):
        for half in (0, 1):
            self.copies.arrive(("2f", half, d1), self.part(half, d1, 2))
        return [(half, d1, 2) for half in (0, 1)]


class Scatter:
    def __init__(self, terms, relays, halves, relay2, halves2, out, copies):
        self.terms, self.relays, self.halves = terms, relays, halves
        self.relay2, self.halves2, self.out, self.copies = relay2, halves2, out, copies
        self.rows = terms.shape[1]

    def part(self, half, df, ds, quarter=None):
        count = self.rows // 2
        first = half * count
        if quarter is not None:
            count = count // 2
            first = first + quarter * count
        slot = place(df, ds) if half == 0 else place(ds, df)
        return self.terms.at[slot, pl.ds(first, count)]

    def relay_send(self, ds):
        for half in (0, 1):
            axis = axes_of(half, False)[0]
            for quarter, step in ((0, 1), (1, -1)):
                self.copies.start(
                    ("1r", half, ds),
                    axis,
                    step,
                    self.part(half, 2, ds, quarter),
                    self.relays.at[half, ds % RING, quarter],
                )

    def near_send(self, ds):
        for half in (0, 1):
            axis = axes_of(half, False)[0]
            self.copies.arrive(("1r", half, ds), self.relays.at[half, ds % RING])
            for quarter, step in ((0, 1), (1, -1)):
                own = self.part(half, step, ds, quarter)
                added = self.relays[half, ds % RING, quarter].astype(jnp.float32)
                own[...] = (own[...].astype(jnp.float32) + added).astype(jnp.bfloat16)
                self.copies.start(
                    ("1", half, ds),
                    axis,
                    step,
                    self.part(half, step, ds),
                    self.halves.at[half, ds % RING, quarter],
                )

    def line_sum(self, ds):
        for half in (0, 1):
            self.copies.arrive(("1", half, ds), self.halves.at[half, ds % RING])
            own = self.part(half, 0, ds)
            total = own[...].astype(jnp.float32)
            for side in (0, 1):
                total = total + self.halves[half, ds % RING, side].astype(jnp.float32)
            own[...] = total.astype(jnp.bfloat16)

    def relay_send2(self):
        for half in (0, 1):
            axis = axes_of(half, False)[1]
            for quarter, step in ((0, 1), (1, -1)):
                self.copies.start(
                    ("2r", half),
                    axis,
                    step,
                    self.part(half, 0, 2, quarter),
                    self.relay2.at[half, quarter],
                )

    def near_send2(self):
        for half in (0, 1):
            axis = axes_of(half, False)[1]
            self.copies.arrive(("2r", half), self.relay2.at[half])
            for quarter, step in ((0, 1), (1, -1)):
                own = self.part(half, 0, step, quarter)
                added = self.relay2[half, quarter].astype(jnp.float32)
                own[...] = (own[...].astype(jnp.float32) + added).astype(jnp.bfloat16)
                self.copies.start(
                    ("2", half),
                    axis,
                    step,
                    self.part(half, 0, step),
                    self.halves2.at[half, quarter],
                )

    def finish(self):
        count = self.rows // 2
        for half in (0, 1):
            self.copies.arrive(("2", half), self.halves2.at[half])
            total = self.part(half, 0, 0)[...].astype(jnp.float32)
            for side in (0, 1):
                total = total + self.halves2[half, side].astype(jnp.float32)
            self.out[pl.ds(half * count, count)] = total.astype(jnp.bfloat16)


def partner():
    me = lax.axis_index("tp")
    return me + 1 - 2 * (me % SPLIT)


def greet_all(near):
    barrier = pltpu.get_barrier_semaphore()
    group = lax.axis_index("grp")
    for device in near.values():
        pl.semaphore_signal(barrier, inc=1, device_id={"tp": device}, device_id_type=MESH)
    for step in range(1, GROUPS):
        other = (group + step) % GROUPS
        pl.semaphore_signal(barrier, inc=1, device_id={"grp": other}, device_id_type=MESH)
    pl.semaphore_wait(barrier, len(near) + GROUPS - 1)


ORDER = (
    ((2, 2),),
    ((2, -1), (-1, 2)),
    ((2, 1), (1, 2)),
    ((2, 0), (0, 2)),
    ((-1, -1), (-1, 1), (1, -1), (1, 1)),
    ((-1, 0), (1, 0), (0, -1), (0, 1)),
    ((0, 0),),
)


def lane_turn(values):
    half = HEAD_DIM // 2
    return jnp.concatenate([values[:, half:], values[:, :half]], 1)


def turn_tables(positions, frequency):
    angles = positions * frequency
    lanes = lax.broadcasted_iota(jnp.int32, angles.shape, 1)
    sine = jnp.sin(angles)
    return jnp.cos(angles), jnp.where(lanes < HEAD_DIM // 2, -sine, sine)


def turn(values, cosine, sine):
    return (values * cosine + lane_turn(values) * sine).astype(jnp.bfloat16)


def dot_rows(left, right):
    return lax.dot_general(
        left, right, (((1,), (1,)), ((), ())), preferred_element_type=jnp.float32
    )


def dot(left, right):
    return jnp.dot(left, right, preferred_element_type=jnp.float32)


def layer_kernel(names, *refs):
    r = types.SimpleNamespace(**dict(zip(names, refs)))
    near = neighbours()
    me = lax.axis_index("tp")
    group = lax.axis_index("grp")
    member = me % SPLIT
    pre_x, dec_x = r.pre_x, r.dec_x
    span, depth = pre_x.shape
    rows = dec_x.shape[0]
    decode = rows // 2
    dec_dev = decode // SPLIT
    wide = r.w_query.shape[1]
    heads_dev = wide // HEAD_DIM
    pre_rows = r.prior_hbm.shape[0]
    pool_pages = r.pool_hbm.shape[0]
    scale = HEAD_DIM ** (-0.5)

    loads, out_loads = {}, {}
    order = ((0, 0), (0, -1), (0, 1), (-1, 0), (1, 0), (0, 2), (2, 0), (-1, -1), (-1, 1), (1, -1))
    order += ((1, 1), (2, -1), (2, 1), (-1, 2), (1, 2), (2, 2))
    order = [place(*offset) for offset in order]
    weights, out_weights = r.weights, r.out_weights
    for slot in order:
        origin = absolute(slot // RING, slot % RING)
        span_rows = pl.ds(pl.multiple_of(origin * depth, depth), depth)
        loads[slot] = (
            pltpu.make_async_copy(
                r.w_query.at[span_rows],
                weights.at[slot, :, pl.ds(0, wide)],
                r.load.at[slot],
            ),
            pltpu.make_async_copy(
                r.w_keyval.at[span_rows],
                weights.at[slot, :, pl.ds(wide, HEAD_DIM)],
                r.load.at[slot],
            ),
        )
    for slot in order:
        origin = absolute(slot // RING, slot % RING)
        columns = pl.ds(pl.multiple_of(origin * depth, depth), depth)
        out_loads[slot] = pltpu.make_async_copy(
            r.w_out.at[:, columns], out_weights.at[slot], r.out_load.at[slot]
        )
    prior_load = pltpu.make_async_copy(r.prior_hbm, r.prior, r.other_load.at[0])
    pre_load = pltpu.make_async_copy(pre_x, r.pre_held.at[0], r.other_load.at[1])
    dec_load = pltpu.make_async_copy(dec_x, r.dec_held.at[0], r.other_load.at[2])
    pool_loads = []
    for part in range(4):
        pages = pl.ds(part * pool_pages // 4, pool_pages // 4)
        pool_loads.append(
            pltpu.make_async_copy(r.pool_hbm.at[pages], r.pool.at[pages], r.other_load.at[3])
        )
    small_loads = [
        pltpu.make_async_copy(source, target, r.other_load.at[4 + index])
        for index, (source, target) in enumerate(
            (
                (r.span_index_hbm, r.span_index),
                (r.assignment_hbm, r.assignment),
                (r.frequency_hbm, r.frequency),
                (r.prefix_pages_hbm, r.prefix_pages),
                (r.decode_len_hbm, r.decode_len),
                (r.page_order_hbm, r.page_order),
            )
        )
    ]
    pre_load.start()
    dec_load.start()
    for copy in small_loads:
        copy.start()
    for slot in order[:5]:
        for copy in loads[slot]:
            copy.start()
    waiting = [copy for slot in order[5:] for copy in loads[slot]]
    waiting += pool_loads + [prior_load] + [out_loads[place(*d)] for d in sum(ORDER, ())]

    def load_more(count):
        for copy in waiting[:count]:
            copy.start()
        del waiting[:count]

    greet_all(near)
    loaded = set()

    def multiply(gather, total, parts):
        for half, d1, d2 in parts:
            slot = gather.slot(half, d1, d2)
            if slot not in loaded:
                loaded.add(slot)
                await_bytes(weights.at[slot], r.load.at[slot])
            count = gather.rows // 2
            at = pl.ds(half * count, count)
            product = dot(gather.part(half, d1, d2)[...], weights[slot])
            if slot == 0:
                total[at] = product
            else:
                total[at] += product

    pre = Gather(pre_x, r.pre_held, Copies(near, r.send.at[0], r.gather_receive.at[0]))
    dec = Gather(dec_x, r.dec_held, Copies(near, r.send.at[1], r.gather_receive.at[1]))
    pre_total, dec_total = r.pre_total, r.dec_total
    pre_load.wait()
    pre.first_sends()
    load_more(4)
    multiply(pre, pre_total, [(0, 0, 0), (1, 0, 0)])

    for copy in small_loads:
        copy.wait()

    span_of = [r.span_index[s] for s in range(GROUPS)]
    goes_to = [r.assignment[s] for s in range(GROUPS)]
    to_here, owner = [], []
    rank = 0 * group
    for s in range(GROUPS):
        here = jnp.where((span_of[s] == SPANS - 1) & (goes_to[s] == group), 1, 0)
        to_here.append(here)
        owner.append((rank & 1) * dec_dev + (rank >> 1))
        rank = rank + here
    start_row = r.span_index[group] * span
    frequency = r.frequency[...]

    def prior_mask():
        live_pages = start_row // PAGE
        column_page = lax.broadcasted_iota(jnp.int32, (1, pre_rows), 1) // PAGE

        def mark(index, live):
            page = r.prefix_pages[0, index]
            page = jnp.where(index < live_pages, page, -1)
            return jnp.where(column_page == page, 0.0, live)

        live = jnp.full((1, pre_rows), masked_score, jnp.float32)
        r.prior_bias[...] = lax.fori_loop(0, pre_rows // PAGE, mark, live, unroll=8)

    def pre_tables():
        spots = (start_row + lax.broadcasted_iota(jnp.int32, (span, HEAD_DIM), 0)).astype(
            jnp.float32
        )
        cosine, sine = turn_tables(spots, frequency)
        r.pre_cos[...] = cosine
        r.pre_sin[...] = sine

    def dec_tables():
        row = lax.broadcasted_iota(jnp.int32, (rows, HEAD_DIM), 0)
        sequence = row % decode

        def spread(index, base):
            length = r.decode_len[0, index // dec_dev, index % dec_dev]
            return jnp.where(sequence == index, length, base)

        base = lax.fori_loop(0, decode, spread, jnp.zeros_like(row), unroll=4)
        taken = jnp.zeros(row.shape, jnp.float32)
        for s in range(GROUPS):
            mine = jnp.where(to_here[s] == 1, owner[s], -1)
            taken = jnp.where(sequence == mine, 1.0, taken)
        base = jnp.where(taken > 0.5, pre_rows + span, base)
        cosine, sine = turn_tables((base + row // decode).astype(jnp.float32), frequency)
        r.dec_cos[...] = cosine
        r.dec_sin[...] = sine
        r.taken[...] = taken
        row = lax.broadcasted_iota(jnp.int32, (STEP_ROWS, rows), 0)
        column = lax.broadcasted_iota(jnp.int32, (STEP_ROWS, rows), 1)
        for s in range(GROUPS):
            mine = jnp.where(to_here[s] == 1, owner[s], -rows)
            picked = (column == row * decode + mine) & (row < 2)
            r.picks[pl.ds(s * STEP_ROWS, STEP_ROWS)] = jnp.where(picked, 1.0, 0.0).astype(
                jnp.bfloat16
            )

    pieces = 8
    chunk = pool_pages // pieces

    def reorder(piece):
        def move(index, carry):
            page = r.page_order[0, member, index]
            r.pages[index] = r.pool[page]
            return carry

        lax.fori_loop(piece * chunk, (piece + 1) * chunk, move, 0, unroll=4)

    pre_tables()
    load_more(6)
    multiply(pre, pre_total, pre.near_arrive())
    prior_mask()
    load_more(6)
    multiply(pre, pre_total, pre.far_arrive())
    dec_tables()
    for d1 in (0, -1, 1, 2):
        parts = pre.line_arrive(d1)
        load_more(4)
        if d1 == 2:
            dec_load.wait()
            dec.first_sends()
        multiply(pre, pre_total, parts)
    multiply(dec, dec_total, [(0, 0, 0), (1, 0, 0)])
    await_bytes(r.pool, r.other_load.at[3])
    r.pages[pl.ds(pool_pages, MAX_PAGES)] = jnp.zeros(
        (MAX_PAGES, PAGE, 2 * HEAD_DIM), jnp.bfloat16
    )
    for index, d1 in enumerate((0, -1, 1, 2)):
        multiply(pre, pre_total, pre.last_arrive(d1))
        load_more(3)
        reorder(2 * index)
        reorder(2 * index + 1)
    load_more(len(waiting))

    def swap(kind, source, target, device):
        pltpu.make_async_remote_copy(
            src_ref=source,
            dst_ref=target,
            send_sem=r.small_send.at[kind],
            recv_sem=r.small_receive.at[kind],
            device_id=device,
            device_id_type=MESH,
        ).start()

    def swapped(kind, region):
        await_bytes(region, r.small_receive.at[kind])

    pre_swap, dec_swap, query_swap, visit_swap, take_swap, back_swap = range(6)
    others = pl.ds(1, GROUPS - 1)
    beside = {"tp": partner()}
    pre_pair, dec_pair = r.pre_pair, r.dec_pair
    pre_pair[member] = pre_total[:, wide:].astype(jnp.bfloat16)
    swap(pre_swap, pre_pair.at[member], pre_pair.at[member], beside)
    cosine, sine = r.pre_cos[...], r.pre_sin[...]
    for head in range(heads_dev):
        at = pl.ds(head * HEAD_DIM, HEAD_DIM)
        r.pre_query[:, at] = turn(pre_total[:, at], cosine, sine)
    dec_parts = dec.near_arrive()
    multiply(dec, dec_total, dec_parts)
    swapped(pre_swap, pre_pair.at[1 - member])
    r.pre_key[...] = turn(
        pre_pair[0].astype(jnp.float32), r.pre_cos[...], r.pre_sin[...]
    )
    prior_load.wait()
    prior_bias = r.prior_bias
    prior = r.prior
    block = span // 2

    def attend(head, part):
        at = pl.ds(head * HEAD_DIM, HEAD_DIM)
        here = pl.ds(part * block, block)
        query = r.pre_query[here, at]
        prior_scores = dot_rows(query, prior[:, pl.ds(0, HEAD_DIM)]) * scale + prior_bias[...]
        own_scores = dot_rows(query, r.pre_key[...]) * scale
        row = lax.broadcasted_iota(jnp.int32, own_scores.shape, 0) + part * block
        column = lax.broadcasted_iota(jnp.int32, own_scores.shape, 1)
        own_scores = jnp.where(row >= column, own_scores, masked_score)
        highest = jnp.maximum(
            jnp.max(prior_scores, 1, keepdims=True), jnp.max(own_scores, 1, keepdims=True)
        )
        prior_raised = jnp.exp(prior_scores - highest)
        own_raised = jnp.exp(own_scores - highest)
        total = jnp.sum(prior_raised, 1, keepdims=True) + jnp.sum(own_raised, 1, keepdims=True)
        values = dot(prior_raised.astype(jnp.bfloat16), prior[:, pl.ds(HEAD_DIM, HEAD_DIM)])
        values = values + dot(own_raised.astype(jnp.bfloat16), pre_pair[1])
        r.pre_heads[here, at] = (values / total).astype(jnp.bfloat16)

    def terms(heads, kept, blocks):
        for dz, dx in blocks:
            slot = place(dz, dx)
            if slot not in term_loaded:
                term_loaded.add(slot)
                out_loads[slot].wait()
            kept[slot] = dot(heads[...], out_weights[slot]).astype(jnp.bfloat16)

    term_loaded = set()
    pre_scatter = Scatter(
        r.pre_terms,
        r.pre_relays,
        r.pre_halves,
        r.pre_relay2,
        r.pre_halves2,
        r.pre_result,
        Copies(near, r.send.at[2], r.scatter_receive.at[0]),
    )
    dec_scatter = Scatter(
        r.dec_terms,
        r.dec_relays,
        r.dec_halves,
        r.dec_relay2,
        r.dec_halves2,
        r.dec_result,
        Copies(near, r.send.at[3], r.scatter_receive.at[1]),
    )
    pre_heads, pre_terms = r.pre_heads, r.pre_terms
    work = [(head, part) for head in range(heads_dev) for part in (0, 1)]
    events = [dec.far_arrive]
    events += [functools.partial(dec.line_arrive, d1) for d1 in (0, -1, 1, 2)]
    for index, item in enumerate(work):
        if index < len(events):
            multiply(dec, dec_total, events[index]())
        attend(*item)
    terms(pre_heads, pre_terms, sum(ORDER, ()))
    for d1 in (0, -1, 1, 2):
        if d1 == 1:
            pre_scatter.relay_send(2)
            pre_scatter.relay_send(-1)
        multiply(dec, dec_total, dec.last_arrive(d1))

    dec_pair[member] = dec_total[:, wide:].astype(jnp.bfloat16)
    swap(dec_swap, dec_pair.at[member], dec_pair.at[member], beside)
    cosine, sine = r.dec_cos[...], r.dec_sin[...]
    for head in range(heads_dev):
        at = pl.ds(head * HEAD_DIM, HEAD_DIM)
        r.steps[:, at] = turn(dec_total[:, at], cosine, sine)

    def of_member(t, which):
        return pl.ds(pl.multiple_of(t * decode + which * dec_dev, dec_dev), dec_dev)

    for t in (0, 1):
        swap(
            query_swap,
            r.steps.at[of_member(t, 1 - member), pl.ds(0, wide)],
            r.seq_query.at[member, t],
            beside,
        )
        r.seq_query[member, t] = r.steps[of_member(t, member), pl.ds(0, wide)]

    pre_scatter.relay_send(1)
    pre_scatter.relay_send(0)
    pre_scatter.near_send(2)

    swapped(dec_swap, dec_pair.at[1 - member])
    r.steps[:, pl.ds(wide, HEAD_DIM)] = turn(
        dec_pair[0].astype(jnp.float32), r.dec_cos[...], r.dec_sin[...]
    )
    r.steps[:, pl.ds(wide + HEAD_DIM, HEAD_DIM)] = dec_pair[1]
    r.visit_out[...] = dot(r.picks[...], r.steps[...]).astype(jnp.bfloat16)
    for step in range(1, GROUPS):
        other = (group + step) % GROUPS
        here = pl.ds(pl.multiple_of(other * STEP_ROWS, STEP_ROWS), STEP_ROWS)
        swap(visit_swap, r.visit_out.at[here], r.visit_in.at[step], {"grp": other})
    for t in (0, 1):
        here = pl.ds(t * dec_dev, dec_dev)
        r.seq_key[here] = r.steps[of_member(t, member), pl.ds(wide, HEAD_DIM)].astype(
            jnp.float32
        )
        r.seq_value[here] = r.steps[
            of_member(t, member), pl.ds(wide + HEAD_DIM, HEAD_DIM)
        ].astype(jnp.float32)
    pre_scatter.near_send(-1)
    swapped(query_swap, r.seq_query.at[1 - member])
    for head in range(heads_dev):
        lines = r.seq_query[:, :, :, pl.ds(head * HEAD_DIM, HEAD_DIM)]
        r.seq_rows[pl.ds(head * rows, rows)] = lines.reshape(rows, HEAD_DIM).astype(jnp.float32)

    counts = [
        (r.decode_len[0, member, index] + (PAGE - 1)) >> 4 for index in range(dec_dev)
    ]
    firsts, total_pages = [], 0
    for index in range(dec_dev):
        firsts.append(total_pages)
        total_pages = total_pages + counts[index]

    def cached_some(part):
        sequences = range(part * dec_dev // 8, (part + 1) * dec_dev // 8)
        lines = [pl.ds(index, 2 * SPLIT * heads_dev, stride=dec_dev) for index in sequences]
        pages = [pl.ds(firsts[index], MAX_PAGES) for index in sequences]
        found = []
        for at, index, here in zip(lines, sequences, pages):
            query = r.seq_rows[at, :]
            keys = r.pages[here, :, pl.ds(0, HEAD_DIM)].reshape(MAX_PAGES * PAGE, HEAD_DIM)
            scores = dot_rows(query.astype(jnp.bfloat16), keys) * scale
            column = lax.broadcasted_iota(jnp.int32, scores.shape, 1)
            scores = jnp.where(column < r.decode_len[0, member, index], scores, masked_score)
            step0 = jnp.sum(query * r.seq_key[pl.ds(index, 1)], 1, keepdims=True) * scale
            step1 = jnp.sum(query * r.seq_key[pl.ds(dec_dev + index, 1)], 1, keepdims=True) * scale
            found.append((scores, step0, step1))
        raised = []
        for scores, step0, step1 in found:
            second = lax.broadcasted_iota(jnp.int32, step1.shape, 0) % 2 == 1
            step1 = jnp.where(second, step1, masked_score)
            highest = jnp.maximum(jnp.max(scores, 1, keepdims=True), jnp.maximum(step0, step1))
            scores = jnp.exp(scores - highest)
            step0 = jnp.exp(step0 - highest)
            step1 = jnp.exp(step1 - highest)
            total = jnp.sum(scores, 1, keepdims=True) + step0 + step1
            raised.append((scores.astype(jnp.bfloat16), step0, step1, total))
        attended = []
        for here, (scores, step0, step1, total) in zip(pages, raised):
            values = r.pages[here, :, pl.ds(HEAD_DIM, HEAD_DIM)]
            attended.append(dot(scores, values.reshape(MAX_PAGES * PAGE, HEAD_DIM)))
        for at, index, values, (scores, step0, step1, total) in zip(
            lines, sequences, attended, raised
        ):
            values = values + step0 * r.seq_value[pl.ds(index, 1)]
            values = values + step1 * r.seq_value[pl.ds(dec_dev + index, 1)]
            r.seq_out[at, :] = values / total

    def visiting():
        swapped(visit_swap, r.visit_in.at[others])
        own = r.visit_out[pl.ds(pl.multiple_of(group * STEP_ROWS, STEP_ROWS), STEP_ROWS)]
        total = own.astype(jnp.float32)
        for step in range(1, GROUPS):
            total = total + r.visit_in[step].astype(jnp.float32)
        query = jnp.concatenate(
            [total[:, head * HEAD_DIM : (head + 1) * HEAD_DIM] for head in range(heads_dev)], 0
        ).astype(jnp.bfloat16)
        new_key = total[:, wide : wide + HEAD_DIM].astype(jnp.bfloat16)
        new_value = total[:, wide + HEAD_DIM :].astype(jnp.bfloat16)
        prior_scores = dot_rows(query, prior[:, pl.ds(0, HEAD_DIM)]) * scale + prior_bias[...]
        own_scores = dot_rows(query, r.pre_key[...]) * scale
        step_scores = dot_rows(query, new_key) * scale
        row = lax.broadcasted_iota(jnp.int32, step_scores.shape, 0) % STEP_ROWS
        column = lax.broadcasted_iota(jnp.int32, step_scores.shape, 1)
        step_scores = jnp.where((column <= row) & (column < 2), step_scores, masked_score)
        highest = jnp.maximum(
            jnp.max(prior_scores, 1, keepdims=True), jnp.max(own_scores, 1, keepdims=True)
        )
        highest = jnp.maximum(highest, jnp.max(step_scores, 1, keepdims=True))
        prior_raised = jnp.exp(prior_scores - highest)
        own_raised = jnp.exp(own_scores - highest)
        step_raised = jnp.exp(step_scores - highest)
        total = jnp.sum(prior_raised, 1, keepdims=True) + jnp.sum(own_raised, 1, keepdims=True)
        total = total + jnp.sum(step_raised, 1, keepdims=True)
        values = dot(prior_raised.astype(jnp.bfloat16), prior[:, pl.ds(HEAD_DIM, HEAD_DIM)])
        values = values + dot(own_raised.astype(jnp.bfloat16), pre_pair[1])
        values = values + dot(step_raised.astype(jnp.bfloat16), new_value)
        values = (values / total).astype(jnp.bfloat16)
        for head in range(heads_dev):
            r.taken_heads[group, :, pl.ds(head * HEAD_DIM, HEAD_DIM)] = values[
                head * STEP_ROWS : (head + 1) * STEP_ROWS
            ]
        for step in range(1, GROUPS):
            other = (group + step) % GROUPS
            swap(take_swap, r.taken_heads.at[group], r.taken_heads.at[group], {"grp": other})

    cached_some(0)
    pre_scatter.near_send(1)
    cached_some(1)
    cached_some(2)
    visiting()
    cached_some(3)
    pre_scatter.line_sum(2)
    pre_scatter.relay_send2()
    cached_some(4)
    cached_some(5)
    cached_some(6)
    cached_some(7)

    for head in range(heads_dev):
        lines = r.seq_out[pl.ds(head * rows, rows)].reshape(SPLIT, 2, dec_dev, HEAD_DIM)
        r.seq_back[:, :, :, pl.ds(head * HEAD_DIM, HEAD_DIM)] = lines.astype(jnp.bfloat16)
    dec_heads = r.dec_heads
    for t in (0, 1):
        swap(
            back_swap,
            r.seq_back.at[1 - member, t],
            dec_heads.at[of_member(t, member)],
            beside,
        )
        dec_heads[of_member(t, member)] = r.seq_back[member, t]
    pre_scatter.near_send(0)
    pre_scatter.line_sum(-1)
    pre_scatter.line_sum(1)
    pre_scatter.near_send2()
    swapped(take_swap, r.taken_heads.at[others])
    placed = lax.dot_general(
        r.picks[...],
        r.taken_heads[...].reshape(GROUPS * STEP_ROWS, wide),
        (((0,), (0,)), ((), ())),
        preferred_element_type=jnp.float32,
    )
    swapped(back_swap, r.seq_back.at[1 - member])
    taken = r.taken[:, 0:1] > 0.5
    r.dec_final[...] = jnp.where(taken, placed, dec_heads[...].astype(jnp.float32)).astype(
        jnp.bfloat16
    )
    dec_final, dec_terms = r.dec_final, r.dec_terms
    for index, ds in enumerate((2, -1, 1, 0)):
        terms(dec_final, dec_terms, ORDER[index])
        dec_scatter.relay_send(ds)
    dec_scatter.near_send(2)
    terms(dec_final, dec_terms, ORDER[4])
    dec_scatter.near_send(-1)
    dec_scatter.near_send(1)
    terms(dec_final, dec_terms, ORDER[5] + ORDER[6])
    pre_scatter.line_sum(0)
    pre_scatter.finish()
    pre_store = pltpu.make_async_copy(r.pre_result, r.pre_out, r.other_load.at[10])
    pre_store.start()
    dec_scatter.line_sum(2)
    dec_scatter.relay_send2()
    dec_scatter.near_send(0)
    dec_scatter.line_sum(-1)
    dec_scatter.line_sum(1)
    dec_scatter.near_send2()
    dec_scatter.line_sum(0)
    dec_scatter.finish()
    dec_store = pltpu.make_async_copy(r.dec_result, r.dec_out, r.other_load.at[11])
    dec_store.start()
    pre_store.wait()
    dec_store.wait()
    rest = pl.ds(1, BLOCKS - 1)
    pre.copies.sent(pre.held.at[rest])
    dec.copies.sent(dec.held.at[rest])
    pre_scatter.copies.sent(pre_terms.at[rest])
    dec_scatter.copies.sent(dec_terms.at[rest])
    for kind, region in (
        (pre_swap, pre_pair.at[member]),
        (dec_swap, dec_pair.at[member]),
        (query_swap, r.seq_query.at[member]),
        (visit_swap, r.visit_in.at[others]),
        (take_swap, r.taken_heads.at[others]),
        (back_swap, r.seq_back.at[member]),
    ):
        await_bytes(region, r.small_send.at[kind])


def scatter_scratch(rows, width):
    half, quarter = rows // 2, rows // 4
    return (
        pltpu.VMEM((BLOCKS, rows, width), jnp.bfloat16),
        pltpu.VMEM((2, RING, 2, quarter, width), jnp.bfloat16),
        pltpu.VMEM((2, RING, 2, half, width), jnp.bfloat16),
        pltpu.VMEM((2, 2, quarter, width), jnp.bfloat16),
        pltpu.VMEM((2, 2, half, width), jnp.bfloat16),
    )


def body(
    prefill_x,
    span_index,
    prefix_pages,
    prefix_cache,
    decode_x,
    decode_len,
    page_order,
    assignment,
    kv_cache,
    w_query,
    w_keyval,
    w_out,
):
    span, depth = prefill_x.shape
    decode = decode_x.shape[1]
    rows = 2 * decode
    dec_dev = decode // SPLIT
    wide = w_query.shape[1]
    both = wide + w_keyval.shape[1]
    carried = wide + 2 * HEAD_DIM
    pre_rows = prefix_cache.shape[2]
    pool_pages = page_order.shape[2]
    exponent = np.arange(HEAD_DIM, dtype=np.float64) % (HEAD_DIM // 2) * (2.0 / HEAD_DIM)
    frequency = (rope_base ** (-exponent)).astype(np.float32)[None, :]
    hbm = pl.BlockSpec(memory_space=pl.ANY)
    operands = dict(
        pre_x=(prefill_x, hbm),
        dec_x=(decode_x.reshape(rows, depth), hbm),
        frequency_hbm=(jnp.asarray(frequency), hbm),
        span_index_hbm=(span_index, hbm),
        assignment_hbm=(assignment, hbm),
        prefix_pages_hbm=(prefix_pages, hbm),
        decode_len_hbm=(decode_len, hbm),
        page_order_hbm=(page_order, hbm),
        w_query=(w_query, hbm),
        w_keyval=(w_keyval, hbm),
        w_out=(w_out, hbm),
        prior_hbm=(prefix_cache.reshape(pre_rows, 2 * HEAD_DIM), hbm),
        pool_hbm=(kv_cache.reshape(pool_pages, PAGE, 2 * HEAD_DIM), hbm),
    )
    results = dict(
        pre_out=jax.ShapeDtypeStruct((span, depth), jnp.bfloat16),
        dec_out=jax.ShapeDtypeStruct((rows, depth), jnp.bfloat16),
    )
    narrow, full = jnp.bfloat16, jnp.float32
    scratch = dict(
        frequency=pltpu.VMEM((1, HEAD_DIM), full),
        span_index=pltpu.SMEM(span_index.shape, jnp.int32),
        assignment=pltpu.SMEM(assignment.shape, jnp.int32),
        prefix_pages=pltpu.SMEM(prefix_pages.shape, jnp.int32),
        decode_len=pltpu.SMEM(decode_len.shape, jnp.int32),
        page_order=pltpu.SMEM(page_order.shape, jnp.int32),
        pre_result=pltpu.VMEM((span, depth), narrow),
        dec_result=pltpu.VMEM((rows, depth), narrow),
        pre_held=pltpu.VMEM((BLOCKS, span, depth), narrow),
        dec_held=pltpu.VMEM((BLOCKS, rows, depth), narrow),
        weights=pltpu.VMEM((BLOCKS, depth, both), narrow),
        out_weights=pltpu.VMEM((BLOCKS, wide, depth), narrow),
        pre_total=pltpu.VMEM((span, both), full),
        dec_total=pltpu.VMEM((rows, both), full),
        pool=pltpu.VMEM((pool_pages, PAGE, 2 * HEAD_DIM), narrow),
        pages=pltpu.VMEM((pool_pages + MAX_PAGES, PAGE, 2 * HEAD_DIM), narrow),
        prior=pltpu.VMEM((pre_rows, 2 * HEAD_DIM), narrow),
        prior_bias=pltpu.VMEM((1, pre_rows), full),
        pre_cos=pltpu.VMEM((span, HEAD_DIM), full),
        pre_sin=pltpu.VMEM((span, HEAD_DIM), full),
        dec_cos=pltpu.VMEM((rows, HEAD_DIM), full),
        dec_sin=pltpu.VMEM((rows, HEAD_DIM), full),
        taken=pltpu.VMEM((rows, HEAD_DIM), full),
        picks=pltpu.VMEM((GROUPS * STEP_ROWS, rows), narrow),
        pre_pair=pltpu.VMEM((SPLIT, span, HEAD_DIM), narrow),
        dec_pair=pltpu.VMEM((SPLIT, rows, HEAD_DIM), narrow),
        pre_query=pltpu.VMEM((span, wide), narrow),
        pre_key=pltpu.VMEM((span, HEAD_DIM), narrow),
        pre_heads=pltpu.VMEM((span, wide), narrow),
        steps=pltpu.VMEM((rows, carried), narrow),
        seq_query=pltpu.VMEM((SPLIT, 2, dec_dev, wide), narrow),
        seq_rows=pltpu.VMEM((rows * wide // HEAD_DIM, HEAD_DIM), full),
        seq_key=pltpu.VMEM((2 * dec_dev, HEAD_DIM), full),
        seq_value=pltpu.VMEM((2 * dec_dev, HEAD_DIM), full),
        seq_out=pltpu.VMEM((rows * wide // HEAD_DIM, HEAD_DIM), full),
        seq_back=pltpu.VMEM((SPLIT, 2, dec_dev, wide), narrow),
        dec_heads=pltpu.VMEM((rows, wide), narrow),
        dec_final=pltpu.VMEM((rows, wide), narrow),
        visit_out=pltpu.VMEM((GROUPS * STEP_ROWS, carried), narrow),
        visit_in=pltpu.VMEM((GROUPS, STEP_ROWS, carried), narrow),
        taken_heads=pltpu.VMEM((GROUPS, STEP_ROWS, wide), narrow),
        **dict(zip(("pre_terms", "pre_relays", "pre_halves", "pre_relay2", "pre_halves2"), scatter_scratch(span, depth))),
        **dict(zip(("dec_terms", "dec_relays", "dec_halves", "dec_relay2", "dec_halves2"), scatter_scratch(rows, depth))),
        load=pltpu.SemaphoreType.DMA((BLOCKS,)),
        out_load=pltpu.SemaphoreType.DMA((BLOCKS,)),
        other_load=pltpu.SemaphoreType.DMA((12,)),
        send=pltpu.SemaphoreType.DMA((4,)),
        gather_receive=pltpu.SemaphoreType.DMA((2, 30)),
        scatter_receive=pltpu.SemaphoreType.DMA((2, 20)),
        small_send=pltpu.SemaphoreType.DMA((6,)),
        small_receive=pltpu.SemaphoreType.DMA((6,)),
    )
    names = tuple(operands) + tuple(results) + tuple(scratch)
    prefill_out, decode_out = pl.pallas_call(
        functools.partial(layer_kernel, names),
        out_shape=tuple(results.values()),
        in_specs=[spec for _, spec in operands.values()],
        out_specs=(hbm, hbm),
        scratch_shapes=list(scratch.values()),
        compiler_params=pltpu.CompilerParams(
            collective_id=0, has_side_effects=True, vmem_limit_bytes=60 * 2**20
        ),
        name="layer",
    )(*(value for value, _ in operands.values()))
    return (prefill_out, decode_out.reshape(2, decode, -1))


def solution(mesh):
    placed = (
        P("grp", "tp"),
        P(),
        P("grp", None),
        P("grp", "tp", None, None),
        P(None, "grp", "tp"),
        P("grp", None, None),
        P("grp", None, None),
        P(),
        P("grp", "tp", None, None),
        P(None, "tp"),
        P(None, "tp"),
        P("tp", None),
    )
    return jax.shard_map(
        body,
        mesh=mesh,
        in_specs=placed,
        out_specs=(P("grp", "tp"), P(None, "grp", "tp")),
        check_vma=False,
    )
```

time: 160 us -> 95.5 us (0.60)
  local copies, waits for them, and re-layouts: 24.3 us -> 3.24 us
  matrix products: 13.3 us -> 0 us
  blocking collectives: 12.6 us -> 0 us
  starting transfers between devices: 8.05 us -> 0 us
  other arithmetic: 5.7 us -> 0 us
  Pallas kernels: 93.8 us -> 91.5 us
    gather x3 -> x0, local copies, waits for them, and re-layouts: 16.6 us -> none  [the longest x1 12 us: body(): cached = pool[page_ids].reshape(dec_dev, MAX_PAGES * PAGE, 2 * HEAD_DIM)]
    dot_general x14 -> x0, matrix products: 13.3 us -> none  [einsum(): return jnp.einsum(form, left, right, preferred_element_type=jnp.float32)]
    all_gather x1 -> x0, blocking collectives: 12.6 us -> none  [body(): taken = lax.all_gather(taken.astype(jnp.bfloat16), 'grp')]
    all_to_all x1 -> x0, starting transfers between devices: 4.47 us -> none  [body(): lax.all_to_all(visiting, 'grp', split_axis=0, concat_axis=0, tiled=True)]
    ppermute x3 -> x0, starting transfers between devices: 3.58 us -> none  [from_partner(): return lax.ppermute(value, axis, pairs)]
    reduce_sum x8 -> x0, other arithmetic: 2.73 us -> none  [the longest x6 2.58 us: joined_softmax(): totals = (jnp.sum(first, -1) + jnp.sum(second, -1))[..., None]]
    pallas_call x2 -> x1, Pallas kernels: 93.8 us -> 91.5 us  [body(): pl.pallas_call(functools.partial(layer_kernel, names), out_shape=tuple(re...]
    unnamed x23 -> x2, local copies, waits for them, and re-layouts: 4.91 us -> 3.24 us
  transfers between devices with their start and end apart: 4 -> 0, of which waited for: 0 -> 0; matrix products, arithmetic and copies ran while one was open for 18% -> 0% of each run, Pallas kernels for 0% -> 0%
where the time goes in v2:
time: 95.5 us; the launch traced here: 95.4 us
  Pallas kernels  91.5 us (96%)
  local copies, waits for them, and re-layouts  3.24 us (3%)
    pallas_call x1, Pallas kernels, body(): pl.pallas_call(functools.partial(layer_kernel, names), out_shape=tuple(re...  91.5 us
    unnamed x2, local copies, waits for them, and re-layouts  3.24 us

profile of v2, /device:TPU:0, one launch (start us, length us, event | category | flops | bytes accessed | tf_op | source)
XLA Modules:
  0.0 95.4 jit_solution(5484974571293250084)
XLA Ops:
  0.6 91.5 %layer.1 = (bf16[256,512]{1,0:T(8,128)(2,1)}, bf16[128,512]{1,0:T(8,128)(2,1)}) custom-call(bf16[256,512]{1,0:T(8,128)(2,1)} %refs_0_.1, bf16[128,512]{1,0:T(8,128)(2,1)} %bitcast.6, f32[1,128]{1,0:T(1,128)} %constant.2.clone.refs_2_, s32[8]{0:T(128)} %refs_3_.1, s32[8]{0:T(128)} %refs_4_.1, s32[1,112]{1,0:T(1,128)} %refs_5_.1, s32[1,2,32]{2,1,0:T(2,128)} %refs_6_.1, ...), custom_call_target="tpu_custom_call" | custom-call | tf_op jit(solution)/shard_map/layer/pallas_call | solution.py:932
  92.2 1.7 %copy.17 = bf16[256,512]{1,0:T(8,128)(2,1)} copy(bf16[256,512]{1,0:T(8,128)(2,1)} %get-tuple-element.8) | data formatting | bytes 524288
  93.8 1.6 %copy.18 = bf16[2,64,512]{2,1,0:T(8,128)(2,1)} copy(bf16[2,64,512]{2,1,0:T(8,128)(2,1)} %bitcast.7) | data formatting | bytes 262144

commit v3 on v2

--- a/solution.py
+++ b/solution.py
@@ -601,10 +601,11 @@
         if index < len(events):
             multiply(dec, dec_total, events[index]())
         attend(*item)
-    terms(pre_heads, pre_terms, sum(ORDER, ()))
     for d1 in (0, -1, 1, 2):
         if d1 == 1:
+            terms(pre_heads, pre_terms, ORDER[0])
             pre_scatter.relay_send(2)
+            terms(pre_heads, pre_terms, ORDER[1])
             pre_scatter.relay_send(-1)
         multiply(dec, dec_total, dec.last_arrive(d1))
 
@@ -627,9 +628,12 @@
         )
         r.seq_query[member, t] = r.steps[of_member(t, member), pl.ds(0, wide)]
 
+    terms(pre_heads, pre_terms, ORDER[2])
     pre_scatter.relay_send(1)
+    terms(pre_heads, pre_terms, ORDER[3])
     pre_scatter.relay_send(0)
     pre_scatter.near_send(2)
+    terms(pre_heads, pre_terms, ORDER[4])
 
     swapped(dec_swap, dec_pair.at[1 - member])
     r.steps[:, pl.ds(wide, HEAD_DIM)] = turn(
@@ -739,6 +743,7 @@
     cached_some(0)
     pre_scatter.near_send(1)
     cached_some(1)
+    terms(pre_heads, pre_terms, ORDER[5] + ORDER[6])
     cached_some(2)
     visiting()
     cached_some(3)

time: 95.5 us -> 92.1 us (0.964)
  Pallas kernels: 91.5 us -> 88.1 us
    pallas_call x1, Pallas kernels: 91.5 us -> 88.1 us  [body(): pl.pallas_call(functools.partial(layer_kernel, names), out_shape=tuple(re...]
where the time goes in v3:
time: 92.1 us; the launch traced here: 92 us
  Pallas kernels  88.1 us (96%)
  local copies, waits for them, and re-layouts  3.24 us (4%)
    pallas_call x1, Pallas kernels, body(): pl.pallas_call(functools.partial(layer_kernel, names), out_shape=tuple(re...  88.1 us
    unnamed x2, local copies, waits for them, and re-layouts  3.24 us

profile of v3, /device:TPU:0, one launch (start us, length us, event | category | flops | bytes accessed | tf_op | source)
XLA Modules:
  0.0 92.0 jit_solution(16198961970358824095)
XLA Ops:
  0.6 88.1 %layer.1 = (bf16[256,512]{1,0:T(8,128)(2,1)}, bf16[128,512]{1,0:T(8,128)(2,1)}) custom-call(bf16[256,512]{1,0:T(8,128)(2,1)} %refs_0_.1, bf16[128,512]{1,0:T(8,128)(2,1)} %bitcast.6, f32[1,128]{1,0:T(1,128)} %constant.2.clone.refs_2_, s32[8]{0:T(128)} %refs_3_.1, s32[8]{0:T(128)} %refs_4_.1, s32[1,112]{1,0:T(1,128)} %refs_5_.1, s32[1,2,32]{2,1,0:T(2,128)} %refs_6_.1, ...), custom_call_target="tpu_custom_call" | custom-call | tf_op jit(solution)/shard_map/layer/pallas_call | solution.py:937
  88.7 1.7 %copy.17 = bf16[256,512]{1,0:T(8,128)(2,1)} copy(bf16[256,512]{1,0:T(8,128)(2,1)} %get-tuple-element.8) | data formatting | bytes 524288
  90.4 1.6 %copy.18 = bf16[2,64,512]{2,1,0:T(8,128)(2,1)} copy(bf16[2,64,512]{2,1,0:T(8,128)(2,1)} %bitcast.7) | data formatting | bytes 262144

commit v4 on v3

--- a/solution.py
+++ b/solution.py
@@ -378,10 +378,10 @@
     dec_load.start()
     for copy in small_loads:
         copy.start()
-    for slot in order[:5]:
+    for slot in order[:1]:
         for copy in loads[slot]:
             copy.start()
-    waiting = [copy for slot in order[5:] for copy in loads[slot]]
+    waiting = [copy for slot in order[1:] for copy in loads[slot]]
     waiting += pool_loads + [prior_load] + [out_loads[place(*d)] for d in sum(ORDER, ())]
 
     def load_more(count):
@@ -411,7 +411,7 @@
     pre_total, dec_total = r.pre_total, r.dec_total
     pre_load.wait()
     pre.first_sends()
-    load_more(4)
+    load_more(12)
     multiply(pre, pre_total, [(0, 0, 0), (1, 0, 0)])
 
     for copy in small_loads:
@@ -597,16 +597,18 @@
     work = [(head, part) for head in range(heads_dev) for part in (0, 1)]
     events = [dec.far_arrive]
     events += [functools.partial(dec.line_arrive, d1) for d1 in (0, -1, 1, 2)]
+    parts = []
     for index, item in enumerate(work):
         if index < len(events):
-            multiply(dec, dec_total, events[index]())
+            parts += events[index]()
         attend(*item)
-    for d1 in (0, -1, 1, 2):
-        if d1 == 1:
-            terms(pre_heads, pre_terms, ORDER[0])
-            pre_scatter.relay_send(2)
-            terms(pre_heads, pre_terms, ORDER[1])
-            pre_scatter.relay_send(-1)
+    parts += dec.last_arrive(0)
+    parts += dec.last_arrive(-1)
+    for index, ds in enumerate((2, -1)):
+        terms(pre_heads, pre_terms, ORDER[index])
+        pre_scatter.relay_send(ds)
+    multiply(dec, dec_total, parts)
+    for d1 in (1, 2):
         multiply(dec, dec_total, dec.last_arrive(d1))
 
     dec_pair[member] = dec_total[:, wide:].astype(jnp.bfloat16)
@@ -821,6 +823,21 @@
         (back_swap, r.seq_back.at[member]),
     ):
         await_bytes(region, r.small_send.at[kind])
+
+
+def results_kernel(pre_from, dec_from, pre_to, dec_to, pre_held, dec_held, done):
+    moves = []
+    for index, (source, held, target) in enumerate(
+        ((pre_from, pre_held, pre_to), (dec_from, dec_held, dec_to))
+    ):
+        fetch = pltpu.make_async_copy(source, held, done.at[0, index])
+        fetch.start()
+        moves.append((fetch, pltpu.make_async_copy(held, target, done.at[1, index])))
+    for fetch, store in moves:
+        fetch.wait()
+        store.start()
+    for _, store in moves:
+        store.wait()
 
 
 def scatter_scratch(rows, width):
@@ -945,6 +962,18 @@
         ),
         name="layer",
     )(*(value for value, _ in operands.values()))
+    prefill_out, decode_out = pl.pallas_call(
+        results_kernel,
+        out_shape=tuple(results.values()),
+        in_specs=[hbm, hbm],
+        out_specs=(hbm, hbm),
+        scratch_shapes=[
+            pltpu.VMEM((span, depth), narrow),
+            pltpu.VMEM((rows, depth), narrow),
+            pltpu.SemaphoreType.DMA((2, 2)),
+        ],
+        name="results",
+    )(prefill_out, decode_out)
     return (prefill_out, decode_out.reshape(2, decode, -1))
 
 

time: 92.1 us -> 89.9 us (0.976)
  local copies, waits for them, and re-layouts: 3.24 us -> 0 us
    unnamed x2 -> x0, local copies, waits for them, and re-layouts: 3.24 us -> none
    pallas_call x0 -> x1, Pallas kernels: none -> 1.73 us  [body(): pl.pallas_call(results_kernel, out_shape=tuple(results.values()), in_spec...]
where the time goes in v4:
time: 89.9 us; the launch traced here: 89.8 us
  Pallas kernels  88.9 us (99%)
    pallas_call x1, Pallas kernels, body(): pl.pallas_call(functools.partial(layer_kernel, names), out_shape=tuple(re...  87.2 us

profile of v4, /device:TPU:0, one launch (start us, length us, event | category | flops | bytes accessed | tf_op | source)
XLA Modules:
  0.0 89.8 jit_solution(9100605882591988647)
XLA Ops:
  0.6 87.2 %layer.1 = (bf16[256,512]{1,0:T(8,128)(2,1)}, bf16[128,512]{1,0:T(8,128)(2,1)}) custom-call(bf16[256,512]{1,0:T(8,128)(2,1)} %refs_0_.1, bf16[128,512]{1,0:T(8,128)(2,1)} %bitcast.6, f32[1,128]{1,0:T(1,128)} %constant.2.clone.refs_2_, s32[8]{0:T(128)} %refs_3_.1, s32[8]{0:T(128)} %refs_4_.1, s32[1,112]{1,0:T(1,128)} %refs_5_.1, s32[1,2,32]{2,1,0:T(2,128)} %refs_6_.1, ...), custom_call_target="tpu_custom_call" | custom-call | tf_op jit(solution)/shard_map/layer/pallas_call | solution.py:954
  87.8 1.7 %results.1 = (bf16[256,512]{1,0:T(8,128)(2,1)}, bf16[128,512]{1,0:T(8,128)(2,1)}) custom-call(bf16[256,512]{1,0:T(8,128)(2,1)} %get-tuple-element.6.pre_from, bf16[128,512]{1,0:T(8,128)(2,1)} %get-tuple-element.7.dec_from), custom_call_target="tpu_custom_call" | custom-call | tf_op jit(solution)/shard_map/results/pallas_call | solution.py:965
